TPU v7x, 128 devices: a whole 4x4x4 slice. The times are simulated.
128 devices in a mesh: line: 16 (over x, y), blk: 8 (over z, core).
Axes of the slice: x: 4, y: 4, z: 4, core: 2. Of those that a mesh axis runs over, the one named last changes fastest.
Arguments:
- state: float32 [5, 512, 128, 128], P(None, 'line', 'blk'), may hold values from -6 to 6
- forcing: float32 [5, 512, 128, 128], P(None, 'line', 'blk'), may hold values from -6 to 6
- viscosity: float32 [5], replicated, may hold values from 0.05 to 0.3
- coupling: float32 [5, 5], replicated, may hold values from -2.5 to 2.5
- thrust: float32 [5], replicated, may hold values from 0.5 to 2
- disk_mask: int32 [512, 128, 128], P('line', 'blk'), may hold values 0 or 1
- block_inverse: float32 [5, 5, 512, 128, 128], P(None, None, 'line', 'blk'), may hold values from -0.12 to 1.4, as said below
- lower_decay: float32 [5, 512, 128, 128], P(None, 'line', 'blk'), may hold values from 0 to 1, as said below
- upper_decay: float32 [5, 512, 128, 128], P(None, 'line', 'blk'), may hold values from 0 to 1, as said below
Outputs:
- update: float32 [5, 512, 128, 128], P(None, 'line', 'blk')
- residual: float32 [5, 512, 128, 128], P(None, 'line', 'blk')
Inputs may be any that keep to these rules, and one draw needn't show every extreme that they name: `block_inverse`: diagonal entries lie between 0.6 and 1.4, the others between -0.12 and 0.12. `lower_decay`: each entry lies strictly between 0 and 1. `upper_decay`: each entry lies strictly between 0 and 1.
All inputs are finite; a program needn't handle non-finite values. No bound on the sum of `disk_mask` on one device may be relied on, other than what follows from the above.
Results may differ from a plain program's by a relative error of at most 0.00023.
Values sent between devices are 32-bit elements; how exact they have to be, the bound alone decides.
A program may use at most 128 MiB of HBM per device.

v0:
```python
import jax
import jax.numpy as jnp
from jax import lax
from jax.sharding import PartitionSpec as P


def with_halo(x, sides, width):
    for axis, dim in sides:
        peers, length = (lax.axis_size(axis), x.shape[dim])
        up = [(i, (i + 1) % peers) for i in range(peers - 1)]
        down = [(j, i) for i, j in up]
        last = lax.slice_in_dim(x, length - width, length, axis=dim)
        first = lax.slice_in_dim(x, 0, width, axis=dim)
        before = lax.ppermute(last, axis, up)
        after = lax.ppermute(first, axis, down)
        x = jnp.concatenate([before, x, after], axis=dim)
    return x


def mix(matrix, field):
    total = matrix[:, 0] * field[0]
    for index in range(1, field.shape[0]):
        total = total + matrix[:, index] * field[index]
    return total


def shifted(values, offset, filler, reverse):
    widths = [(0, 0)] * values.ndim
    if reverse:
        widths[1] = (0, offset)
        return jnp.pad(values[:, offset:], widths, constant_values=filler)
    widths[1] = (offset, 0)
    return jnp.pad(values[:, :-offset], widths, constant_values=filler)


def doubling_scan(decay, value, reverse):
    depth = decay.shape[1]
    offset = 1
    while offset < depth:
        prior_decay = shifted(decay, offset, 1.0, reverse)
        prior_value = shifted(value, offset, 0.0, reverse)
        value = decay * prior_value + value
        decay = prior_decay * decay
        offset = offset * 2
    return (decay, value)


def line_solve(source, lower, upper):
    swept = doubling_scan(lower, jnp.sqrt(1.0 - lower * lower) * source, False)[1]
    return doubling_scan(upper, jnp.sqrt(1.0 - upper * upper) * swept, True)[1]


def solve_pieces(pieces):
    return line_solve(pieces[0], pieces[1], pieces[2])


def local(
    state, forcing, viscosity, coupling, thrust, disk_mask, block_inverse, lower_decay, upper_decay
):
    padded = with_halo(state, (("line", 1), ("blk", 2)), 1)
    beside = padded[:, 2:, 1:-1] + padded[:, :-2, 1:-1] + padded[:, 1:-1, 2:] + padded[:, 1:-1, :-2]
    beside = beside + jnp.roll(state, 1, 3) + jnp.roll(state, -1, 3)
    diffusion = viscosity[:, None, None, None] * (6.0 * state - beside)
    sink = disk_mask.astype(jnp.float32)[None] * thrust[:, None, None, None] * state
    residual = forcing - diffusion - mix(coupling[:, :, None, None, None], state) - sink
    source = mix(block_inverse, residual)
    solved = solve_pieces(
        (
            lax.all_to_all(source, "line", split_axis=2, concat_axis=1, tiled=True),
            lax.all_to_all(lower_decay, "line", split_axis=2, concat_axis=1, tiled=True),
            lax.all_to_all(upper_decay, "line", split_axis=2, concat_axis=1, tiled=True),
        )
    )
    returned = lax.all_to_all(solved, "line", split_axis=1, concat_axis=2, tiled=True)
    return (returned, residual)


def solution(mesh):
    in_specs = (
        P(None, "line", "blk", None),
        P(None, "line", "blk", None),
        P(),
        P(),
        P(),
        P("line", "blk", None),
        P(None, None, "line", "blk", None),
        P(None, "line", "blk", None),
        P(None, "line", "blk", None),
    )
    out_specs = (P(None, "line", "blk", None), P(None, "line", "blk", None))
    return jax.shard_map(local, mesh=mesh, in_specs=in_specs, out_specs=out_specs, check_vma=False)
```

profile of v0, /device:TPU:32, one launch (start us, length us, event | category | flops | bytes accessed | tf_op | source)
XLA Modules:
  0.0 132.3 jit_solution(9881527938891684345)
XLA Ops:
  0.6 1.4 %fusion.22 = (f32[5,1,16,128]{3,2,1,0:T(8,128)S(1)}, f32[5,1,16,128]{3,2,1,0:T(8,128)}) fusion(f32[5,32,16,128]{3,2,1,0:T(8,128)} %param.9), kind=kLoop, calls=%fused_computation.86 | loop fusion | bytes 163840 | tf_op jit(solution)/shard_map/slice | solution.py:12
  2.0 1.3 collective-permute-start
  3.3 4.5 %collective-permute-start.1 = (f32[5,1,16,128]{3,1,2,0:T(1,128)S(1)}, f32[5,1,16,128]{3,1,2,0:T(1,128)S(1)}, u32[]{:S(2)}, u32[]{:S(2)}) collective-permute-start(f32[5,1,16,128]{3,1,2,0:T(1,128)S(1)} %bitcast.109), channel_id=1, source_target_pairs={{0,8},{8,16},{16,24},{24,32},{32,40},{40,48},{48,56},{56,64},{64,7... | collective-permute-start | bytes 122888 | tf_op jit(solution)/shard_map/ppermute | solution.py:14
  7.9 2.9 %copy.62 = f32[5,32,16,128]{3,1,0,2:T(8,128)} copy(f32[5,32,16,128]{3,2,1,0:T(8,128)} %param.16) | data formatting | bytes 2621440 | tf_op args[7]
  10.8 9.1 %all-to-all-start.1 = ((f32[5,32,16,128]{3,1,0,2:T(8,128)}), f32[5,32,16,128]{3,1,0,2:T(8,128)}, u32[]{:S(2)}, u32[]{:S(2)}) async-start(f32[5,32,16,128]{3,1,0,2:T(8,128)} %copy.62), calls=%async_computation.1 | async-start | bytes 2621440 | tf_op jit(solution)/shard_map/all_to_all | solution.py:70
  19.9 0.4 copy.65
  20.4 2.0 %fusion.20 = (f32[5,32,16,127]{3,1,2,0:T(8,128)}, f32[5,32,16,127]{3,1,2,0:T(8,128)}) fusion(f32[5,32,16,128]{3,1,2,0:T(8,128)S(1)} %copy.65), kind=kLoop, calls=%fused_computation.84 | loop fusion | bytes 5201920 | tf_op jit(solution)/shard_map/jit(_roll_static)/slice | solution.py:62
  22.3 1.9 %fusion.21 = (f32[5,32,16,1]{3,1,2,0:T(8,128)}, f32[5,32,16,1]{3,1,2,0:T(8,128)}) fusion(f32[5,32,16,128]{3,1,2,0:T(8,128)S(1)} %copy.65), kind=kLoop, calls=%fused_computation.85 | loop fusion | bytes 40960 | tf_op jit(solution)/shard_map/jit(_roll_static)/slice | solution.py:62
  24.3 2.9 %fusion.19 = (f32[5,1,32,16,128]{4,3,2,1,0:T(8,128)}, f32[5,1,32,16,128]{4,3,2,1,0:T(8,128)}, f32[5,1,32,16,128]{4,3,2,1,0:T(8,128)}, f32[5,1,32,16,128]{4,3,2,1,0:T(8,128)}, f32[5,1,32,16,128]{4,3,2,1,0:T(8,128)}) fusion(f32[5,5,32,16,128]{4,3,2,1,0:T(8,128)S(1)} %bitcast.105), kind=kLoop, calls=%fused_computation.83 | loop fusion | bytes 13107200 | tf_op jit(solution)/shard_map/slice | solution.py:21
  27.6 0.8 copy.79
  28.4 0.8 copy.80
  29.2 0.8 copy.81
  30.0 1.5 %copy.60 = f32[5,32,16,128]{3,1,0,2:T(8,128)} copy(f32[5,32,16,128]{3,2,1,0:T(8,128)S(1)} %copy-done.9) | data formatting | bytes 2621440 | tf_op args[8]
  31.5 0.7 pad_maximum_fusion.10
  32.2 1.9 %collective-permute-start.2 = (f32[5,34,1,128]{3,1,2,0:T(8,128)}, f32[5,34,1,128]{3,1,2,0:T(8,128)}, u32[]{:S(2)}, u32[]{:S(2)}) collective-permute-start(f32[5,34,1,128]{3,1,2,0:T(8,128)} %get-tuple-element.46), channel_id=1, source_target_pairs={{1,0},{2,1},{3,2},{4,3},{5,4},{6,5},{7,6},{9,8},{10,9},{11,10},{12... | collective-permute-start | bytes 261128 | tf_op jit(solution)/shard_map/ppermute | solution.py:15
  34.1 2.4 %collective-permute-start.3 = (f32[5,34,1,128]{3,1,2,0:T(8,128)}, f32[5,34,1,128]{3,1,2,0:T(8,128)}, u32[]{:S(2)}, u32[]{:S(2)}) collective-permute-start(f32[5,34,1,128]{3,1,2,0:T(8,128)} %get-tuple-element.47), channel_id=1, source_target_pairs={{0,1},{1,2},{2,3},{3,4},{4,5},{5,6},{6,7},{8,9},{9,10},{10,11},{11... | collective-permute-start | bytes 261128 | tf_op jit(solution)/shard_map/ppermute | solution.py:14
  36.8 3.3 %all-to-all-done.1 = f32[5,32,16,128]{3,1,0,2:T(8,128)} async-done(((f32[5,32,16,128]{3,1,0,2:T(8,128)}), f32[5,32,16,128]{3,1,0,2:T(8,128)}, u32[]{:S(2)}, u32[]{:S(2)}) %all-to-all-start.1) | async-done | bytes 1310752 | tf_op jit(solution)/shard_map/all_to_all | solution.py:70
  40.1 3.9 %all-to-all-start = ((f32[5,32,16,128]{3,1,0,2:T(8,128)}), f32[5,32,16,128]{3,1,0,2:T(8,128)S(1)}, u32[]{:S(2)}, u32[]{:S(2)}) async-start(f32[5,32,16,128]{3,1,0,2:T(8,128)} %copy.60), calls=%async_computation | async-start | bytes 2621440 | tf_op jit(solution)/shard_map/all_to_all | solution.py:71
  44.0 5.0 %fusion.7 = f32[5,32,16,128]{3,1,2,0:T(8,128)S(1)} fusion(f32[5,34,1,128]{3,1,2,0:T(8,128)} %collective-permute-done.3, f32[5,1,16,128]{3,1,2,0:T(1,128)S(1)} %collective-permute-done, f32[5,32,16,128]{3,1,2,0:T(8,128)S(1)} %copy.65, f32[5,1,16,128]{3,1,2,0:T(1,128)S(1)} %collective-permute-done.1, f32[5,34,1,128]{3,1,2,0:T(8,128)} %collective-permute-done.2, ...), kind=kLoop, calls=%fused_computation.8 | loop fusion | flops 10485760 | bytes 8382604 | tf_op jit(solution)/shard_map/sub | solution.py:65
  49.2 0.9 copy-done
  50.1 0.7 copy-done.3
  50.8 0.4 copy-done.4
  51.2 3.4 %fusion.11 = f32[5,32,16,128]{3,1,0,2:T(8,128)} fusion(f32[5,1,32,16,128]{4,3,2,1,0:T(8,128)S(1)} %copy-done.7, f32[5,1,32,16,128]{4,3,2,1,0:T(8,128)S(1)} %copy-done.4, f32[5,1,32,16,128]{4,3,2,1,0:T(8,128)S(1)} %copy-done.5, f32[5,1,32,16,128]{4,3,2,1,0:T(8,128)S(1)} %copy-done.6, f32[5,1,32,16,128]{4,3,2,1,0:T(8,128)S(1)} %copy-done.3, ...), kind=kLoop, calls=%fused_computation.20 | loop fusion | flops 2949120 | bytes 9175040 | tf_op jit(solution)/shard_map/add | solution.py:23
  54.6 11.5 %all-to-all-done = f32[5,32,16,128]{3,1,0,2:T(8,128)S(1)} async-done(((f32[5,32,16,128]{3,1,0,2:T(8,128)}), f32[5,32,16,128]{3,1,0,2:T(8,128)S(1)}, u32[]{:S(2)}, u32[]{:S(2)}) %all-to-all-start) | async-done | bytes 1310752 | tf_op jit(solution)/shard_map/all_to_all | solution.py:71
  66.0 4.6 %all-to-all-start.2 = ((f32[5,32,16,128]{3,1,0,2:T(8,128)}), f32[5,32,16,128]{3,1,0,2:T(8,128)}, u32[]{:S(2)}, u32[]{:S(2)}) async-start(f32[5,32,16,128]{3,1,0,2:T(8,128)} %fusion.11), calls=%async_computation.2 | async-start | bytes 2621440 | tf_op jit(solution)/shard_map/all_to_all | solution.py:69
  70.8 1.1 slice.272
  71.9 1.4 %copy.63 = f32[5,32,16,128]{3,1,2,0:T(8,128)S(1)} copy(f32[5,32,16,128]{3,1,0,2:T(8,128)} %all-to-all-done.1) | data formatting | bytes 2621440 | tf_op jit(solution)/shard_map/all_to_all | solution.py:70
  73.3 18.9 %all-to-all-done.2 = f32[5,32,16,128]{3,1,0,2:T(8,128)} async-done(((f32[5,32,16,128]{3,1,0,2:T(8,128)}), f32[5,32,16,128]{3,1,0,2:T(8,128)}, u32[]{:S(2)}, u32[]{:S(2)}) %all-to-all-start.2) | async-done | bytes 1310752 | tf_op jit(solution)/shard_map/all_to_all | solution.py:69
  92.3 1.4 %copy.87 = f32[5,32,16,128]{3,1,2,0:T(8,128)S(1)} copy(f32[5,32,16,128]{3,1,0,2:T(8,128)} %all-to-all-done.2) | data formatting | bytes 2621440 | tf_op jit(solution)/shard_map/all_to_all | solution.py:69
  93.7 0.5 bitcast_multiply_fusion
  94.1 0.6 multiply_add_fusion.16
  94.8 0.4 multiply_add_fusion.15
  95.2 0.3 multiply_add_fusion.14
  96.1 0.3 multiply_add_fusion.12
  96.6 0.3 multiply_add_fusion.11
  97.9 0.6 add_multiply_fusion
  98.6 0.3 multiply_add_fusion.8
  99.0 1.2 copy-done.8
  100.2 0.4 multiply_add_fusion.7
  100.8 0.3 multiply_add_fusion.6
  101.7 0.3 multiply_add_fusion.4
  102.3 0.3 multiply_add_fusion.3
  103.6 0.3 multiply_add_fusion
  103.9 2.4 %copy.88 = f32[5,512,1,128]{3,2,0,1:T(1,128)} copy(f32[5,512,1,128]{3,1,0,2:T(8,128)S(1)} %multiply_add_fusion) | data formatting | bytes 2621440 | tf_op jit(solution)/shard_map/add | solution.py:42
  106.3 3.8 %all-to-all-start.3 = ((f32[5,512,1,128]{3,2,0,1:T(1,128)}), f32[5,512,1,128]{3,2,0,1:T(1,128)S(1)}, u32[]{:S(2)}, u32[]{:S(2)}) async-start(f32[5,512,1,128]{3,2,0,1:T(1,128)} %copy.88), calls=%async_computation.3 | async-start | bytes 2621440 | tf_op jit(solution)/shard_map/all_to_all | solution.py:74
  110.1 1.8 %copy.91 = f32[5,32,16,128]{3,2,1,0:T(8,128)} copy(f32[5,32,16,128]{3,1,2,0:T(8,128)S(1)} %copy-done.1) | data formatting | bytes 2621440
  112.0 18.5 %all-to-all-done.3 = f32[5,512,1,128]{3,2,0,1:T(1,128)S(1)} async-done(((f32[5,512,1,128]{3,2,0,1:T(1,128)}), f32[5,512,1,128]{3,2,0,1:T(1,128)S(1)}, u32[]{:S(2)}, u32[]{:S(2)}) %all-to-all-start.3) | async-done | bytes 1310752 | tf_op jit(solution)/shard_map/all_to_all | solution.py:74
  130.5 1.8 %copy.90 = f32[5,32,16,128]{3,2,1,0:T(8,128)} copy(f32[5,32,16,128]{3,1,2,0:T(8,128)S(1)} %bitcast.107) | data formatting | bytes 2621440
  (75 shorter events, 4.7 us)
Async XLA Ops:
  2.0 29.4 %collective-permute-start = (f32[5,1,16,128]{3,1,2,0:T(1,128)}, f32[5,1,16,128]{3,1,2,0:T(1,128)S(1)}, u32[]{:S(2)}, u32[]{:S(2)}) collective-permute-start(f32[5,1,16,128]{3,1,2,0:T(1,128)} %bitcast.11), channel_id=1, source_target_pairs={{8,0},{16,8},{24,16},{32,24},{40,32},{48,40},{56,48},{64,56},{72,6... | collective-permute-start | bytes 122888 | tf_op jit(solution)/shard_map/ppermute | solution.py:15
  3.3 28.1 %collective-permute-start.1 = (f32[5,1,16,128]{3,1,2,0:T(1,128)S(1)}, f32[5,1,16,128]{3,1,2,0:T(1,128)S(1)}, u32[]{:S(2)}, u32[]{:S(2)}) collective-permute-start(f32[5,1,16,128]{3,1,2,0:T(1,128)S(1)} %bitcast.109), channel_id=1, source_target_pairs={{0,8},{8,16},{16,24},{24,32},{32,40},{40,48},{48,56},{56,64},{64,7... | collective-permute-start | bytes 122888 | tf_op jit(solution)/shard_map/ppermute | solution.py:14
  10.8 9.2 %copy-start.2 = (f32[5,32,16,128]{3,2,1,0:T(8,128)S(1)}, f32[5,32,16,128]{3,2,1,0:T(8,128)}, u32[]{:S(2)}) copy-start(f32[5,32,16,128]{3,2,1,0:T(8,128)} %param.9) | copy-start | bytes 3932164
  10.8 29.3 %all-to-all-start.1 = ((f32[5,32,16,128]{3,1,0,2:T(8,128)}), f32[5,32,16,128]{3,1,0,2:T(8,128)}, u32[]{:S(2)}, u32[]{:S(2)}) async-start(f32[5,32,16,128]{3,1,0,2:T(8,128)} %copy.62), calls=%async_computation.1 | async-start | bytes 2621440 | tf_op jit(solution)/shard_map/all_to_all | solution.py:70
  19.9 4.3 %slice-start = ((s8[6553600]{0:T(1024)(128)(4,1)}), s8[4194304]{0:T(1024)(128)(4,1)S(1)}, s32[]{:S(2)}) async-start(s8[6553600]{0:T(1024)(128)(4,1)} %bitcast.104), calls=%async_computation.4 | async-start | bytes 8388608
  20.3 3.9 %slice-start.1 = ((s8[6553600]{0:T(1024)(128)(4,1)}), s8[2359296]{0:T(1024)(128)(4,1)S(1)}, s32[]{:S(2)}) async-start(s8[6553600]{0:T(1024)(128)(4,1)} %bitcast.104), calls=%async_computation.5 | async-start | bytes 4718592
  27.3 1.9 %copy-start.10 = (s32[32,16,128]{2,1,0:T(8,128)S(1)}, s32[32,16,128]{2,1,0:T(8,128)}, u32[]{:S(2)}) copy-start(s32[32,16,128]{2,1,0:T(8,128)} %param.14) | copy-start | bytes 786436
  27.5 2.5 %copy-start.9 = (f32[5,32,16,128]{3,2,1,0:T(8,128)S(1)}, f32[5,32,16,128]{3,2,1,0:T(8,128)}, u32[]{:S(2)}) copy-start(f32[5,32,16,128]{3,2,1,0:T(8,128)} %param.17) | copy-start | bytes 3932164
  31.4 5.1 %copy-start.11 = (f32[5,5]{1,0:T(8,128)S(1)}, f32[5,5]{1,0:T(8,128)}, u32[]{:S(2)}) copy-start(f32[5,5]{1,0:T(8,128)} %param.12) | copy-start | bytes 304
  32.2 11.8 %collective-permute-start.2 = (f32[5,34,1,128]{3,1,2,0:T(8,128)}, f32[5,34,1,128]{3,1,2,0:T(8,128)}, u32[]{:S(2)}, u32[]{:S(2)}) collective-permute-start(f32[5,34,1,128]{3,1,2,0:T(8,128)} %get-tuple-element.46), channel_id=1, source_target_pairs={{1,0},{2,1},{3,2},{4,3},{5,4},{6,5},{7,6},{9,8},{10,9},{11,10},{12... | collective-permute-start | bytes 261128 | tf_op jit(solution)/shard_map/ppermute | solution.py:15
  34.1 9.9 %collective-permute-start.3 = (f32[5,34,1,128]{3,1,2,0:T(8,128)}, f32[5,34,1,128]{3,1,2,0:T(8,128)}, u32[]{:S(2)}, u32[]{:S(2)}) collective-permute-start(f32[5,34,1,128]{3,1,2,0:T(8,128)} %get-tuple-element.47), channel_id=1, source_target_pairs={{0,1},{1,2},{2,3},{3,4},{4,5},{5,6},{6,7},{8,9},{9,10},{10,11},{11... | collective-permute-start | bytes 261128 | tf_op jit(solution)/shard_map/ppermute | solution.py:14
  36.7 7.2 %copy-start.12 = (f32[5]{0:T(128)S(1)}, f32[5]{0:T(128)}, u32[]{:S(2)}) copy-start(f32[5]{0:T(128)} %param.13) | copy-start | bytes 64
  36.7 7.2 %copy-start.13 = (f32[5]{0:T(128)S(1)}, f32[5]{0:T(128)}, u32[]{:S(2)}) copy-start(f32[5]{0:T(128)} %param.11) | copy-start | bytes 64
  40.1 26.0 %all-to-all-start = ((f32[5,32,16,128]{3,1,0,2:T(8,128)}), f32[5,32,16,128]{3,1,0,2:T(8,128)S(1)}, u32[]{:S(2)}, u32[]{:S(2)}) async-start(f32[5,32,16,128]{3,1,0,2:T(8,128)} %copy.60), calls=%async_computation | async-start | bytes 2621440 | tf_op jit(solution)/shard_map/all_to_all | solution.py:71
  44.0 6.1 %copy-start.5 = (f32[5,1,32,16,128]{4,3,2,1,0:T(8,128)S(1)}, f32[5,1,32,16,128]{4,3,2,1,0:T(8,128)}, u32[]{:S(2)}) copy-start(f32[5,1,32,16,128]{4,3,2,1,0:T(8,128)} %get-tuple-element.43) | copy-start | bytes 3932164
  44.0 6.1 %copy-start.6 = (f32[5,1,32,16,128]{4,3,2,1,0:T(8,128)S(1)}, f32[5,1,32,16,128]{4,3,2,1,0:T(8,128)}, u32[]{:S(2)}) copy-start(f32[5,1,32,16,128]{4,3,2,1,0:T(8,128)} %get-tuple-element.44) | copy-start | bytes 3932164
  44.0 6.1 %copy-start.7 = (f32[5,1,32,16,128]{4,3,2,1,0:T(8,128)S(1)}, f32[5,1,32,16,128]{4,3,2,1,0:T(8,128)}, u32[]{:S(2)}) copy-start(f32[5,1,32,16,128]{4,3,2,1,0:T(8,128)} %get-tuple-element.45) | copy-start | bytes 3932164
  49.0 1.1 copy-start
  49.0 1.8 %copy-start.3 = (f32[5,1,32,16,128]{4,3,2,1,0:T(8,128)S(1)}, f32[5,1,32,16,128]{4,3,2,1,0:T(8,128)}, u32[]{:S(2)}) copy-start(f32[5,1,32,16,128]{4,3,2,1,0:T(8,128)} %get-tuple-element.41) | copy-start | bytes 3932164
  49.0 2.2 %copy-start.4 = (f32[5,1,32,16,128]{4,3,2,1,0:T(8,128)S(1)}, f32[5,1,32,16,128]{4,3,2,1,0:T(8,128)}, u32[]{:S(2)}) copy-start(f32[5,1,32,16,128]{4,3,2,1,0:T(8,128)} %get-tuple-element.42) | copy-start | bytes 3932164
  66.0 26.2 %all-to-all-start.2 = ((f32[5,32,16,128]{3,1,0,2:T(8,128)}), f32[5,32,16,128]{3,1,0,2:T(8,128)}, u32[]{:S(2)}, u32[]{:S(2)}) async-start(f32[5,32,16,128]{3,1,0,2:T(8,128)} %fusion.11), calls=%async_computation.2 | async-start | bytes 2621440 | tf_op jit(solution)/shard_map/all_to_all | solution.py:69
  98.9 1.3 copy-start.8
  106.3 3.8 %copy-start.1 = (f32[5,32,16,128]{3,1,2,0:T(8,128)S(1)}, f32[5,32,16,128]{3,1,2,0:T(8,128)}, u32[]{:S(2)}) copy-start(f32[5,32,16,128]{3,1,2,0:T(8,128)} %copy-done) | copy-start | bytes 3932164
  106.3 24.1 %all-to-all-start.3 = ((f32[5,512,1,128]{3,2,0,1:T(1,128)}), f32[5,512,1,128]{3,2,0,1:T(1,128)S(1)}, u32[]{:S(2)}, u32[]{:S(2)}) async-start(f32[5,512,1,128]{3,2,0,1:T(1,128)} %copy.88), calls=%async_computation.3 | async-start | bytes 2621440 | tf_op jit(solution)/shard_map/all_to_all | solution.py:74
where the time goes:
time: 133 us; the launch traced here: 132 us
  waiting for transfers between devices  52.2 us (39%)
  local copies, waits for them, and re-layouts  31.6 us (24%)
  starting transfers between devices  31.6 us (24%)
  other arithmetic  15.7 us (12%)
    all_to_all x1, waiting for transfers between devices, local(): lax.all_to_all(source, 'line', split_axis=2, concat_axis=1, tiled=True)  18.9 us
    all_to_all x1, waiting for transfers between devices, local(): lax.all_to_all(solved, 'line', split_axis=1, concat_axis=2, tiled=True)  18.5 us
    unnamed x37, local copies, waits for them, and re-layouts  11.7 us
    all_to_all x1, waiting for transfers between devices, local(): lax.all_to_all(upper_decay, 'line', split_axis=2, concat_axis=1, tiled=True)  11.5 us
    all_to_all x1, starting transfers between devices, local(): lax.all_to_all(lower_decay, 'line', split_axis=2, concat_axis=1, tiled=True)  9.14 us
    ppermute x2, starting transfers between devices, with_halo(): before = lax.ppermute(last, axis, up)  6.96 us
    add x17, other arithmetic, doubling_scan(): value = decay * prior_value + value  5.49 us
    sub x1, other arithmetic, local(): forcing - diffusion - mix(coupling[:, :, None, None, None], state) - sink  4.99 us
  transfers between devices with their start and end apart: 8, of which 4 were waited for; matrix products, arithmetic and copies ran while one was open for 21% of the time, Pallas kernels for 0%

commit v1 on v0

v1 whole, which is shorter than its diff:
```python
import jax
import jax.numpy as jnp
from jax import lax
from jax.experimental import pallas as pl
from jax.experimental.pallas import tpu as pltpu
from jax.sharding import PartitionSpec as P

F = 5
NV = 2 * F
CH = 4


def kernel(
    visc_h, coup_h, thr_h, state_h, forcing_h, mask_h, binv_h, lower_h, upper_h,
    update_h, resid_h,
    st, fo, mk, bi, lo, up, gl, gu, qg, rr, vv, sw,
    visc, coup, thr, xs, xh, acd_s, acd_r, be_s, be_r, ret_s, ret_r,
    load_sem, small_sem, chunk_sem, halo_ssem, halo_rsem,
    acd_ssem, acd_rsem, be_ssem, be_rsem, ret_ssem, ret_rsem, out_sem,
):
    n_line = lax.axis_size("line")
    n_blk = lax.axis_size("blk")
    me = lax.axis_index("line")
    mb = lax.axis_index("blk")
    depth = lo.shape[1]
    step = depth // CH

    def load(src, dst, sem):
        return pltpu.make_async_copy(src, dst, sem)

    ld_state = load(state_h, st.at[:, pl.ds(1, depth)], load_sem.at[0])
    ld_lower = load(lower_h, lo, load_sem.at[1])
    ld_upper = load(upper_h, up, load_sem.at[2])
    ld_small = [
        load(src, dst, small_sem.at[i])
        for i, (src, dst) in enumerate(((visc_h, visc), (coup_h, coup), (thr_h, thr)))
    ]
    ld_state.start()
    ld_lower.start()
    ld_upper.start()

    def chunk_loads(k):
        part = pl.ds(k * step, step)
        return (
            load(forcing_h.at[:, part], fo.at[:, part], chunk_sem.at[0, k]),
            load(mask_h.at[part], mk.at[part], chunk_sem.at[1, k]),
            load(binv_h.at[:, :, part], bi.at[:, :, part], chunk_sem.at[2, k]),
        )

    for cp in ld_small:
        cp.start()

    for k in range(CH):
        for cp in chunk_loads(k):
            cp.start()

    barrier = pltpu.get_barrier_semaphore()

    def greet(d, c):
        pl.semaphore_signal(barrier, inc=1, device_id={"line": lax.rem(me + d, n_line)})
        return c

    lax.fori_loop(1, n_line, greet, 0)

    @pl.when(mb > 0)
    def _():
        pl.semaphore_signal(barrier, inc=1, device_id={"blk": mb - 1})

    @pl.when(mb < n_blk - 1)
    def _():
        pl.semaphore_signal(barrier, inc=1, device_id={"blk": mb + 1})

    ld_state.wait()

    for c in range(F):
        for side, row in ((0, 0), (1, 15)):
            xs[side, c] = st[c, 1 : depth + 1, row, :]

    beside_blk = jnp.where(mb > 0, 1, 0) + jnp.where(mb < n_blk - 1, 1, 0)
    pl.semaphore_wait(barrier, n_line - 1 + beside_blk)

    def z_send(side):
        to = me - 1 if side == 0 else me + 1
        src = st.at[:, 1] if side == 0 else st.at[:, depth]
        dst = st.at[:, depth + 1] if side == 0 else st.at[:, 0]
        return pltpu.make_async_remote_copy(
            src_ref=src, dst_ref=dst, send_sem=halo_ssem.at[side], recv_sem=halo_rsem.at[side],
            device_id={"line": to},
        )

    def x_send(side):
        to = mb - 1 if side == 0 else mb + 1
        return pltpu.make_async_remote_copy(
            src_ref=xs.at[side], dst_ref=xh.at[1 - side],
            send_sem=halo_ssem.at[2 + side], recv_sem=halo_rsem.at[2 + side],
            device_id={"blk": to},
        )

    zeros_plane = jnp.zeros((F, 16, 128), jnp.float32)
    zeros_side = jnp.zeros((F, depth, 128), jnp.float32)

    @pl.when(mb > 0)
    def _():
        x_send(0).start()

    @pl.when(mb < n_blk - 1)
    def _():
        x_send(1).start()

    @pl.when(me > 0)
    def _():
        z_send(0).start()

    @pl.when(me < n_line - 1)
    def _():
        z_send(1).start()

    @pl.when(mb == 0)
    def _():
        xh[0] = zeros_side

    @pl.when(mb == n_blk - 1)
    def _():
        xh[1] = zeros_side

    @pl.when(me == 0)
    def _():
        st[:, 0] = zeros_plane

    @pl.when(me == n_line - 1)
    def _():
        st[:, depth + 1] = zeros_plane

    ld_lower.wait()
    ld_upper.wait()
    ones = jnp.ones((F, 16, 128), jnp.float32)

    def early_up(z, carry):
        p, q = carry
        l = lo[:, z]
        u = up[:, z]
        l2 = 1.0 - l * l
        u2 = 1.0 - u * u
        g = u2 * lax.rsqrt(u2)
        gl[:, z] = l2 * lax.rsqrt(l2)
        gu[:, z] = g
        p = p * l
        rr[:, z] = g * p
        qg[:, z] = q * g
        return p, q * u

    p_all, _ = lax.fori_loop(0, depth, early_up, (ones, ones))

    def early_down(i, carry):
        r, v = carry
        z = depth - 1 - i
        u = up[:, z]
        r = u * r + rr[:, z]
        v = u * v
        rr[:, z] = r
        vv[:, z] = v
        return r, v

    d_all, c_all = lax.fori_loop(0, depth, early_down, (jnp.zeros_like(ones), ones))

    for i, val in enumerate((p_all, c_all, d_all)):
        for c in range(F):
            for h in range(2):
                acd_s[2 * c + h, i] = val[c, 8 * h : 8 * h + 8]

    def acd_copy(j):
        return pltpu.make_async_remote_copy(
            src_ref=acd_s.at[j], dst_ref=acd_r.at[me], send_sem=acd_ssem.at[j], recv_sem=acd_rsem,
            device_id={"line": j},
        )

    def be_copy(j):
        return pltpu.make_async_remote_copy(
            src_ref=be_s.at[j], dst_ref=be_r.at[me], send_sem=be_ssem.at[j], recv_sem=be_rsem,
            device_id={"line": j},
        )

    def to_solvers(action):
        def one(d, c):
            j = lax.rem(me + d, n_line)

            @pl.when(j < NV)
            def _():
                action(j)

            return c

        lax.fori_loop(1, n_line, one, 0)

    to_solvers(lambda j: acd_copy(j).start())

    @pl.when(me < NV)
    def _():
        acd_r[me] = acd_s[me]

    @pl.when(mb > 0)
    def _():
        x_send(1).wait_recv()

    @pl.when(mb < n_blk - 1)
    def _():
        x_send(0).wait_recv()

    @pl.when(me > 0)
    def _():
        z_send(1).wait_recv()

    @pl.when(me < n_line - 1)
    def _():
        z_send(0).wait_recv()

    rows = lax.broadcasted_iota(jnp.int32, (8, 128), 0)
    first = rows == 0
    last = rows == 7
    for cp in ld_small:
        cp.wait()
    vis = [visc[c] for c in range(F)]
    thrust = [thr[c] for c in range(F)]
    mat = [[coup[c, d] + 6.0 * vis[c] if c == d else coup[c, d] for d in range(F)] for c in range(F)]

    def residual_copy(k):
        part = pl.ds(k * step, step)
        return pltpu.make_async_copy(fo.at[:, part], resid_h.at[:, part], out_sem.at[0, k])

    def cell(z, carry):
        s, e = carry
        cen = [[st[c, z + 1, 8 * h : 8 * h + 8, :] for h in range(2)] for c in range(F)]
        m = [mk[z, 8 * h : 8 * h + 8, :].astype(jnp.float32) for h in range(2)]
        res = []
        for c in range(F):
            v0, v1 = cen[c]
            r0, r1 = pltpu.roll(v0, 1, 0), pltpu.roll(v1, 1, 0)
            q0, q1 = pltpu.roll(v0, 7, 0), pltpu.roll(v1, 7, 0)
            before = jnp.broadcast_to(xh[0, c, pl.ds(z, 1), :], (8, 128))
            after = jnp.broadcast_to(xh[1, c, pl.ds(z, 1), :], (8, 128))
            xsum = (
                jnp.where(first, before, r0) + jnp.where(last, q1, q0),
                jnp.where(first, r0, r1) + jnp.where(last, after, q1),
            )
            pair = []
            for h in range(2):
                sub = slice(8 * h, 8 * h + 8)
                v = cen[c][h]
                beside = st[c, z, sub, :] + st[c, z + 2, sub, :]
                beside = beside + (pltpu.roll(v, 1, 1) + pltpu.roll(v, 127, 1))
                beside = beside + xsum[h]
                total = (mat[c][c] + m[h] * thrust[c]) * v
                for d in range(F):
                    if d != c:
                        total = total + mat[c][d] * cen[d][h]
                r = (fo[c, z, sub, :] + vis[c] * beside) - total
                fo[c, z, sub, :] = r
                pair.append(r)
            res.append(pair)
        new_s, new_e = [], []
        for c in range(F):
            for h in range(2):
                sub = slice(8 * h, 8 * h + 8)
                src = bi[c, 0, z, sub, :] * res[0][h]
                for d in range(1, F):
                    src = src + bi[c, d, z, sub, :] * res[d][h]
                v = lo[c, z, sub, :] * s[2 * c + h] + gl[c, z, sub, :] * src
                sw[c, z, sub, :] = v
                new_s.append(v)
                new_e.append(e[2 * c + h] + qg[c, z, sub, :] * v)
        return tuple(new_s), tuple(new_e)

    def chunk(k, carry):
        for cp in chunk_loads(k):
            cp.wait()
        carry = lax.fori_loop(k * step, (k + 1) * step, cell, carry)
        residual_copy(k).start()
        return carry

    zero = tuple(jnp.zeros((8, 128), jnp.float32) for _ in range(NV))
    b_all, e_all = lax.fori_loop(0, CH, chunk, (zero, zero))
    for v in range(NV):
        be_s[v, 0] = b_all[v]
        be_s[v, 1] = e_all[v]
    to_solvers(lambda j: be_copy(j).start())

    def ret_copy(k):
        return pltpu.make_async_remote_copy(
            src_ref=ret_s.at[k], dst_ref=ret_r.at[me], send_sem=ret_ssem.at[k], recv_sem=ret_rsem,
            device_id={"line": k},
        )

    @pl.when(me < NV)
    def _():
        be_r[me] = be_s[me]

    def back(i, u):
        z = depth - 1 - i
        u = up[:, z] * u + gu[:, z] * sw[:, z]
        sw[:, z] = u
        return u

    lax.fori_loop(0, depth, back, jnp.zeros_like(ones))

    def drain(ref, sem):
        pltpu.make_async_copy(ref, ref, sem).wait()

    @pl.when(me < NV)
    def _():
        drain(acd_r.at[pl.ds(0, n_line - 1)], acd_rsem)
        drain(be_r.at[pl.ds(0, n_line - 1)], be_rsem)
        s = jnp.zeros((8, 128), jnp.float32)
        t = []
        for k in range(n_line):
            ret_s[k, 0] = s
            t.append(acd_r[k, 2] * s + be_r[k, 1])
            s = acd_r[k, 0] * s + be_r[k, 0]
        u = jnp.zeros((8, 128), jnp.float32)
        for k in range(n_line - 1, -1, -1):
            ret_s[k, 1] = u
            u = acd_r[k, 1] * u + t[k]

        def answer(d, c):
            ret_copy(lax.rem(me + d, n_line)).start()
            return c

        lax.fori_loop(1, n_line, answer, 0)
        ret_r[me] = ret_s[me]
        drain(ret_r.at[pl.ds(0, NV - 1)], ret_rsem)

    @pl.when(me >= NV)
    def _():
        drain(ret_r.at[pl.ds(0, NV)], ret_rsem)

    def update_copy(k):
        part = pl.ds(k * step, step)
        return pltpu.make_async_copy(sw.at[:, part], update_h.at[:, part], out_sem.at[1, k])

    s_in = jnp.stack([jnp.concatenate([ret_r[2 * c, 0], ret_r[2 * c + 1, 0]], axis=0) for c in range(F)])
    u_in = jnp.stack([jnp.concatenate([ret_r[2 * c, 1], ret_r[2 * c + 1, 1]], axis=0) for c in range(F)])

    def finish(k, c):
        def one(z, c):
            sw[:, z] = sw[:, z] + rr[:, z] * s_in + vv[:, z] * u_in
            return c

        lax.fori_loop(k * step, (k + 1) * step, one, 0)
        update_copy(k).start()
        return c

    lax.fori_loop(0, CH, finish, 0)

    @pl.when(mb > 0)
    def _():
        x_send(0).wait_send()

    @pl.when(mb < n_blk - 1)
    def _():
        x_send(1).wait_send()

    @pl.when(me > 0)
    def _():
        z_send(0).wait_send()

    @pl.when(me < n_line - 1)
    def _():
        z_send(1).wait_send()

    to_solvers(lambda j: acd_copy(j).wait_send())
    to_solvers(lambda j: be_copy(j).wait_send())

    @pl.when(me < NV)
    def _():
        def done(d, c):
            ret_copy(lax.rem(me + d, n_line)).wait_send()
            return c

        lax.fori_loop(1, n_line, done, 0)

    for k in range(CH):
        residual_copy(k).wait()
        update_copy(k).wait()


def local(
    state, forcing, viscosity, coupling, thrust, disk_mask, block_inverse, lower_decay, upper_decay
):
    fields, depth, width, lanes = state.shape
    n_line = lax.axis_size("line")
    full = (fields, depth, width, lanes)
    f32 = jnp.float32
    V = pltpu.VMEM
    dma = pltpu.SemaphoreType.DMA
    hbm = pl.BlockSpec(memory_space=pltpu.HBM)
    return pl.pallas_call(
        kernel,
        out_shape=(pltpu.HBM(full, f32), pltpu.HBM(full, f32)),
        in_specs=[hbm] * 9,
        out_specs=(hbm, hbm),
        scratch_shapes=[
            V((fields, depth + 2, width, lanes), f32),
            V(full, f32),
            V((depth, width, lanes), jnp.int32),
            V((fields,) + full, f32),
            V(full, f32),
            V(full, f32),
            V(full, f32),
            V(full, f32),
            V(full, f32),
            V(full, f32),
            V(full, f32),
            V(full, f32),
            pltpu.SMEM((fields,), f32),
            pltpu.SMEM((fields, fields), f32),
            pltpu.SMEM((fields,), f32),
            V((2, fields, depth, lanes), f32),
            V((2, fields, depth, lanes), f32),
            V((NV, 3, 8, lanes), f32),
            V((n_line, 3, 8, lanes), f32),
            V((NV, 2, 8, lanes), f32),
            V((n_line, 2, 8, lanes), f32),
            V((n_line, 2, 8, lanes), f32),
            V((NV, 2, 8, lanes), f32),
            dma((3,)),
            dma((3,)),
            dma((3, CH)),
            dma((4,)),
            dma((4,)),
            dma((NV,)),
            dma,
            dma((NV,)),
            dma,
            dma((n_line,)),
            dma,
            dma((2, CH)),
        ],
        compiler_params=pltpu.CompilerParams(
            collective_id=0, has_side_effects=True, vmem_limit_bytes=48 * 1024 * 1024
        ),
    )(
        *(
            pltpu.with_memory_space_constraint(x, pltpu.HBM)
            for x in (
                viscosity, coupling, thrust, state, forcing, disk_mask, block_inverse, lower_decay, upper_decay
            )
        )
    )


def solution(mesh):
    in_specs = (
        P(None, "line", "blk", None),
        P(None, "line", "blk", None),
        P(),
        P(),
        P(),
        P("line", "blk", None),
        P(None, None, "line", "blk", None),
        P(None, "line", "blk", None),
        P(None, "line", "blk", None),
    )
    out_specs = (P(None, "line", "blk", None), P(None, "line", "blk", None))
    return jax.shard_map(local, mesh=mesh, in_specs=in_specs, out_specs=out_specs, check_vma=False)
```

time: 133 us -> 28.7 us (0.22)
  the two profiles are of different devices: /device:TPU:32 before, /device:TPU:1 now
where the time goes in v1:
time: 28.7 us; the launch traced here: 28.3 us
  Pallas kernels  23.9 us (83%)
  local copies, waits for them, and re-layouts  3.67 us (13%)
  between operations  0.65 us (2%)
    pallas_call x1, Pallas kernels, local(): pl.pallas_call(kernel, out_shape=(pltpu.HBM(full, f32), pltpu.HBM(full, f...  23.9 us
    unnamed x4, local copies, waits for them, and re-layouts  3.67 us

profile of v1, /device:TPU:1, one launch (start us, length us, event | category | flops | bytes accessed | tf_op | source)
XLA Modules:
  0.0 28.3 jit_solution(13723565620917666719)
XLA Ops:
  0.6 23.9 %shard_map.104 = (f32[5,32,16,128]{3,2,1,0:T(8,128)}, f32[5,32,16,128]{3,2,1,0:T(8,128)}) custom-call(f32[5]{0:T(128)} %visc_h.1, f32[5,5]{1,0:T(8,128)} %coup_h.1, f32[5]{0:T(128)} %thr_h.1, f32[5,32,16,128]{3,2,1,0:T(8,128)} %state_h.1, f32[5,32,16,128]{3,2,1,0:T(8,128)} %forcing_h.1, s32[32,16,128]{2,1,0:T(8,128)} %mask_h.1, ...), custom_call_target="tpu_custom_call" | custom-call | tf_op jit(solution)/shard_map/pallas_call | solution.py:395
  24.6 0.0 copy-start
  24.6 2.6 %copy.13 = f32[5,32,16,128]{3,2,1,0:T(8,128)} copy(f32[5,32,16,128]{3,2,1,0:T(8,128)} %get-tuple-element.4) | data formatting | bytes 2621440
  27.2 0.0 copy-done
  27.2 1.1 %copy.14 = f32[5,32,16,128]{3,2,1,0:T(8,128)} copy(f32[5,32,16,128]{3,2,1,0:T(8,128)S(1)} %copy-done) | data formatting | bytes 2621440
Async XLA Ops:
  24.6 2.6 %copy-start = (f32[5,32,16,128]{3,2,1,0:T(8,128)S(1)}, f32[5,32,16,128]{3,2,1,0:T(8,128)}, u32[]{:S(2)}) copy-start(f32[5,32,16,128]{3,2,1,0:T(8,128)} %get-tuple-element.5) | copy-start | bytes 3932164

commit v2 on v0

v2 whole, which is shorter than its diff:
```python
import jax
import jax.numpy as jnp
from jax import lax
from jax.experimental import pallas as pl
from jax.experimental.pallas import tpu as pltpu
from jax.sharding import PartitionSpec as P

F = 5
NV = 2 * F
CH = 4
UE = 2
UR = 2
US = 2
UB = 2
HALF = (slice(0, 8), slice(8, 16))


def planes(begin, count, unroll, body, carry, down=False):
    def some(i, carry):
        for j in range(unroll):
            z = i * unroll + j
            carry = body(begin - z if down else begin + z, carry)
        return carry

    return lax.fori_loop(0, count // unroll, some, carry)


def tiles(fn):
    return tuple(fn(c, h) for c in range(F) for h in range(2))


def segment_kernel(
    visc_h, coup_h, thr_h, state_h, forcing_h, mask_h, binv_h, lower_h, upper_h,
    u0, rr, vv, fo, ret,
    st, mk, bi, lo, up, gl, gu, qg, pp, sw,
    visc, coup, thr, xs, xh, zh, acd_s, acd_r, be_s, be_r, ret_s, ret_r,
    small_sem, load_sem, binv_sem, halo_ssem, halo_rsem,
    acd_ssem, acd_rsem, be_ssem, be_rsem, ret_ssem, ret_rsem,
):
    n_line = lax.axis_size("line")
    n_blk = lax.axis_size("blk")
    me = lax.axis_index("line")
    mb = lax.axis_index("blk")
    depth = lo.shape[1]
    step = depth // CH

    copy = pltpu.make_async_copy
    ld_state = copy(state_h, st.at[:, pl.ds(1, depth)], load_sem.at[0])
    ld_forcing = copy(forcing_h, fo, load_sem.at[1])
    ld_mask = copy(mask_h, mk, load_sem.at[2])
    ld_lower = copy(lower_h, lo, load_sem.at[3])
    ld_upper = copy(upper_h, up, load_sem.at[4])
    ld_small = [
        copy(src, dst, small_sem.at[i])
        for i, (src, dst) in enumerate(((visc_h, visc), (coup_h, coup), (thr_h, thr)))
    ]

    def ld_binv(k):
        part = pl.ds(k * step, step)
        return copy(binv_h.at[:, :, part], bi.at[:, :, part], binv_sem.at[k])

    ld_state.start()
    for cp in ld_small:
        cp.start()
    ld_forcing.start()
    ld_mask.start()
    ld_lower.start()
    ld_upper.start()

    def ahead(d):
        j = me + d
        return jnp.where(j >= n_line, j - n_line, j)

    barrier = pltpu.get_barrier_semaphore()
    for d in range(1, n_line):
        pl.semaphore_signal(barrier, inc=1, device_id={"line": ahead(d)})

    @pl.when(mb > 0)
    def _():
        pl.semaphore_signal(barrier, inc=1, device_id={"blk": mb - 1})

    @pl.when(mb < n_blk - 1)
    def _():
        pl.semaphore_signal(barrier, inc=1, device_id={"blk": mb + 1})

    for k in range(CH):
        ld_binv(k).start()

    zero_tile = jnp.zeros((8, 128), jnp.float32)
    one_tile = jnp.ones((8, 128), jnp.float32)
    for c in range(F):
        for sub in HALF:
            st[c, 0, sub, :] = zero_tile
            st[c, depth + 1, sub, :] = zero_tile

    ld_state.wait()
    for c in range(F):
        for side, row in ((0, 0), (1, 15)):
            xs[side, c] = st[c, 1 : depth + 1, row, :]

    beside_blk = jnp.where(mb > 0, 1, 0) + jnp.where(mb < n_blk - 1, 1, 0)
    pl.semaphore_wait(barrier, n_line - 1 + beside_blk)

    def z_send(side):
        return pltpu.make_async_remote_copy(
            src_ref=st.at[:, depth if side else 1], dst_ref=zh.at[1 - side],
            send_sem=halo_ssem.at[side], recv_sem=halo_rsem.at[side],
            device_id={"line": me + 1 if side else me - 1},
        )

    def x_send(side):
        return pltpu.make_async_remote_copy(
            src_ref=xs.at[side], dst_ref=xh.at[1 - side],
            send_sem=halo_ssem.at[2 + side], recv_sem=halo_rsem.at[2 + side],
            device_id={"blk": mb + 1 if side else mb - 1},
        )

    has_low, has_high = me > 0, me < n_line - 1
    has_left, has_right = mb > 0, mb < n_blk - 1
    halos = (
        (has_left, x_send(0), x_send(1)),
        (has_right, x_send(1), x_send(0)),
        (has_low, z_send(0), z_send(1)),
        (has_high, z_send(1), z_send(0)),
    )
    for cond, out, _ in halos:
        pl.when(cond)(out.start)

    ld_forcing.wait()
    ld_mask.wait()
    for cp in ld_small:
        cp.wait()
    rows = lax.broadcasted_iota(jnp.int32, (8, 128), 0)
    first = rows == 0
    last = rows == 7
    vis = [visc[c] for c in range(F)]
    mat = [[-coup[c, d] for d in range(F)] for c in range(F)]
    plain = [mat[c][c] - 6.0 * vis[c] for c in range(F)]
    sunk = [plain[c] - thr[c] for c in range(F)]

    def residual_plane(z, carry):
        cen = [[st[c, z + 1, sub, :] for sub in HALF] for c in range(F)]
        disk = [mk[z, sub, :] != 0 for sub in HALF]
        for c in range(F):
            v0, v1 = cen[c]
            r0, r1 = pltpu.roll(v0, 1, 0), pltpu.roll(v1, 1, 0)
            q0, q1 = pltpu.roll(v0, 7, 0), pltpu.roll(v1, 7, 0)
            xsum = (
                jnp.where(first, 0.0, r0) + jnp.where(last, q1, q0),
                jnp.where(first, r0, r1) + jnp.where(last, 0.0, q1),
            )
            for h, sub in enumerate(HALF):
                v = cen[c][h]
                beside = (st[c, z, sub, :] + st[c, z + 2, sub, :]) + xsum[h]
                beside = beside + (pltpu.roll(v, 1, 1) + pltpu.roll(v, 127, 1))
                total = fo[c, z, sub, :] + vis[c] * beside
                total = total + jnp.where(disk[h], sunk[c], plain[c]) * v
                for d in range(F):
                    if d != c:
                        total = total + mat[c][d] * cen[d][h]
                fo[c, z, sub, :] = total
        return carry

    planes(0, depth, UR, residual_plane, 0)

    ld_lower.wait()
    ld_upper.wait()

    def decay_plane(z, carry):
        new = []
        for i, (p, q, r) in enumerate(carry):
            c, sub = i // 2, HALF[i % 2]
            l, u = lo[c, z, sub, :], up[c, z, sub, :]
            l2 = 1.0 - l * l
            u2 = 1.0 - u * u
            g = u2 * lax.rsqrt(u2)
            gl[c, z, sub, :] = l2 * lax.rsqrt(l2)
            gu[c, z, sub, :] = g
            p = p * l
            w = q * g
            pp[c, z, sub, :] = p
            qg[c, z, sub, :] = w
            new.append((p, q * u, r + w * p))
        return tuple(new)

    acd = planes(0, depth, UE, decay_plane, ((one_tile, one_tile, zero_tile),) * NV)
    for v in range(NV):
        for i in range(3):
            acd_s[v, i] = acd[v][i]

    def to_solvers(src, dst, ssem, rsem):
        for d in range(1, n_line):
            j = ahead(d)

            @pl.when(j < NV)
            def _():
                pltpu.make_async_remote_copy(
                    src_ref=src.at[j], dst_ref=dst.at[me], send_sem=ssem, recv_sem=rsem,
                    device_id={"line": j},
                ).start()

    def drain(ref, sem):
        copy(ref, ref, sem).wait()

    to_solvers(acd_s, acd_r, acd_ssem, acd_rsem)

    pl.when(has_left)(halos[0][2].wait_recv)
    pl.when(has_right)(halos[1][2].wait_recv)
    pl.when(has_low)(halos[2][2].wait_recv)
    pl.when(has_high)(halos[3][2].wait_recv)

    def add_x(side, row):
        for c in range(F):
            fo[c, :, row, :] = fo[c, :, row, :] + vis[c] * xh[side, c]

    def add_z(side, z):
        for c in range(F):
            fo[c, z] = fo[c, z] + vis[c] * zh[side, c]

    pl.when(has_left)(lambda: add_x(0, 0))
    pl.when(has_right)(lambda: add_x(1, 15))
    pl.when(has_low)(lambda: add_z(0, 0))
    pl.when(has_high)(lambda: add_z(1, depth - 1))

    def sweep_plane(z, carry):
        s, e = carry
        new_s, new_e = [], []
        for i in range(NV):
            c, sub = i // 2, HALF[i % 2]
            src = bi[c, 0, z, sub, :] * fo[0, z, sub, :]
            for d in range(1, F):
                src = src + bi[c, d, z, sub, :] * fo[d, z, sub, :]
            v = lo[c, z, sub, :] * s[i] + gl[c, z, sub, :] * src
            sw[c, z, sub, :] = v
            new_s.append(v)
            new_e.append(e[i] + qg[c, z, sub, :] * v)
        return tuple(new_s), tuple(new_e)

    carry = ((zero_tile,) * NV, (zero_tile,) * NV)

    def sweep_chunk(k, carry):
        ld_binv(k).wait()
        return planes(k * step, step, US, sweep_plane, carry)

    b_all, e_all = lax.fori_loop(0, CH, sweep_chunk, carry)
    for v in range(NV):
        be_s[v, 0] = b_all[v]
        be_s[v, 1] = e_all[v]
    to_solvers(be_s, be_r, be_ssem, be_rsem)

    def down_plane(z, carry):
        new = []
        for i, (u, r, v) in enumerate(carry):
            c, sub = i // 2, HALF[i % 2]
            a, g = up[c, z, sub, :], gu[c, z, sub, :]
            u = a * u + g * sw[c, z, sub, :]
            r = a * r + g * pp[c, z, sub, :]
            v = a * v
            u0[c, z, sub, :] = u
            rr[c, z, sub, :] = r
            vv[c, z, sub, :] = v
            new.append((u, r, v))
        return tuple(new)

    planes(depth - 1, depth, UB, down_plane, ((zero_tile, zero_tile, one_tile),) * NV, down=True)

    @pl.when(me < NV)
    def _():
        acd_r[me] = acd_s[me]
        be_r[me] = be_s[me]
        drain(acd_r.at[pl.ds(0, n_line - 1)], acd_rsem)
        drain(be_r.at[pl.ds(0, n_line - 1)], be_rsem)
        s = zero_tile
        t = []
        for k in range(n_line):
            ret_s[k, 0] = s
            t.append(acd_r[k, 2] * s + be_r[k, 1])
            s = acd_r[k, 0] * s + be_r[k, 0]
        u = zero_tile
        for k in range(n_line - 1, -1, -1):
            ret_s[k, 1] = u
            u = acd_r[k, 1] * u + t[k]
        for d in range(1, n_line):
            k = ahead(d)
            pltpu.make_async_remote_copy(
                src_ref=ret_s.at[k], dst_ref=ret_r.at[me], send_sem=ret_ssem, recv_sem=ret_rsem,
                device_id={"line": k},
            ).start()
        ret_r[me] = ret_s[me]
        drain(acd_s.at[pl.ds(0, NV - 1)], acd_ssem)
        drain(be_s.at[pl.ds(0, NV - 1)], be_ssem)
        drain(ret_s.at[pl.ds(0, n_line - 1)], ret_ssem)
        drain(ret_r.at[pl.ds(0, NV - 1)], ret_rsem)

    @pl.when(me >= NV)
    def _():
        drain(acd_s, acd_ssem)
        drain(be_s, be_ssem)
        drain(ret_r, ret_rsem)

    for v in range(NV):
        for i in range(2):
            ret[v, i] = ret_r[v, i]

    for cond, out, _ in halos:
        pl.when(cond)(out.wait_send)


def finish_kernel(u0, rr, vv, fo, ret, update_h, resid_h, out, res_sem, out_sem):
    depth = u0.shape[1]
    step = depth // CH
    write_res = pltpu.make_async_copy(fo, resid_h, res_sem)
    write_res.start()

    def update_copy(k):
        part = pl.ds(k * step, step)
        return pltpu.make_async_copy(out.at[:, part], update_h.at[:, part], out_sem.at[k])

    s_in = tiles(lambda c, h: ret[2 * c + h, 0])
    u_in = tiles(lambda c, h: ret[2 * c + h, 1])

    def plane(z, carry):
        for i in range(NV):
            c, sub = i // 2, HALF[i % 2]
            out[c, z, sub, :] = u0[c, z, sub, :] + rr[c, z, sub, :] * s_in[i] + vv[c, z, sub, :] * u_in[i]
        return carry

    for k in range(CH):
        planes(k * step, step, 2, plane, 0)
        update_copy(k).start()
    write_res.wait()
    for k in range(CH):
        update_copy(k).wait()


def local(
    state, forcing, viscosity, coupling, thrust, disk_mask, block_inverse, lower_decay, upper_decay
):
    fields, depth, width, lanes = state.shape
    n_line = lax.axis_size("line")
    full = (fields, depth, width, lanes)
    f32 = jnp.float32
    V = pltpu.VMEM
    dma = pltpu.SemaphoreType.DMA
    hbm = pl.BlockSpec(memory_space=pltpu.HBM)
    vmem = pl.BlockSpec(memory_space=pltpu.VMEM)
    args = (viscosity, coupling, thrust, state, forcing, disk_mask, block_inverse, lower_decay, upper_decay)
    parts = pl.pallas_call(
        segment_kernel,
        out_shape=(V(full, f32),) * 4 + (V((NV, 2, 8, lanes), f32),),
        in_specs=[hbm] * len(args),
        out_specs=(vmem,) * 5,
        scratch_shapes=[
            V((fields, depth + 2, width, lanes), f32),
            V((depth, width, lanes), jnp.int32),
            V((fields,) + full, f32),
            V(full, f32),
            V(full, f32),
            V(full, f32),
            V(full, f32),
            V(full, f32),
            V(full, f32),
            V(full, f32),
            pltpu.SMEM((fields,), f32),
            pltpu.SMEM((fields, fields), f32),
            pltpu.SMEM((fields,), f32),
            V((2, fields, depth, lanes), f32),
            V((2, fields, depth, lanes), f32),
            V((2, fields, width, lanes), f32),
            V((NV, 3, 8, lanes), f32),
            V((n_line, 3, 8, lanes), f32),
            V((NV, 2, 8, lanes), f32),
            V((n_line, 2, 8, lanes), f32),
            V((n_line, 2, 8, lanes), f32),
            V((NV, 2, 8, lanes), f32),
            dma((3,)),
            dma((5,)),
            dma((CH,)),
            dma((4,)),
            dma((4,)),
            dma, dma, dma, dma, dma, dma,
        ],
        compiler_params=pltpu.CompilerParams(
            collective_id=0, has_side_effects=True, vmem_limit_bytes=40 * 1024 * 1024
        ),
    )(*(pltpu.with_memory_space_constraint(x, pltpu.HBM) for x in args))
    return pl.pallas_call(
        finish_kernel,
        out_shape=(pltpu.HBM(full, f32), pltpu.HBM(full, f32)),
        in_specs=[vmem] * 5,
        out_specs=(hbm, hbm),
        scratch_shapes=[V(full, f32), dma, dma((CH,))],
        compiler_params=pltpu.CompilerParams(vmem_limit_bytes=16 * 1024 * 1024),
    )(*(pltpu.with_memory_space_constraint(x, pltpu.VMEM) for x in parts))


def solution(mesh):
    in_specs = (
        P(None, "line", "blk", None),
        P(None, "line", "blk", None),
        P(),
        P(),
        P(),
        P("line", "blk", None),
        P(None, None, "line", "blk", None),
        P(None, "line", "blk", None),
        P(None, "line", "blk", None),
    )
    out_specs = (P(None, "line", "blk", None), P(None, "line", "blk", None))
    return jax.shard_map(local, mesh=mesh, in_specs=in_specs, out_specs=out_specs, check_vma=False)
```

time: 133 us -> 22.1 us (0.17)
  the two profiles are of different devices: /device:TPU:32 before, /device:TPU:1 now
where the time goes in v2:
time: 22.1 us; the launch traced here: 21.9 us
  Pallas kernels  21.2 us (96%)
  between operations  0.64 us (3%)
    pallas_call x1, Pallas kernels, local(): pl.pallas_call(segment_kernel, out_shape=(V(full, f32),) * 4 + (V((NV, 2,...  19.7 us
    pallas_call x1, Pallas kernels, local(): pl.pallas_call(finish_kernel, out_shape=(pltpu.HBM(full, f32), pltpu.HBM(...  1.52 us

profile of v2, /device:TPU:1, one launch (start us, length us, event | category | flops | bytes accessed | tf_op | source)
XLA Modules:
  0.0 21.9 jit_solution(395466886942964536)
XLA Ops:
  0.6 19.7 %shard_map.104 = (f32[5,32,16,128]{3,2,1,0:T(8,128)S(1)}, f32[5,32,16,128]{3,2,1,0:T(8,128)S(1)}, f32[5,32,16,128]{3,2,1,0:T(8,128)S(1)}, f32[5,32,16,128]{3,2,1,0:T(8,128)S(1)}, f32[10,2,8,128]{3,2,1,0:T(8,128)S(1)}) custom-call(f32[5]{0:T(128)} %visc_h.1, f32[5,5]{1,0:T(8,128)} %coup_h.1, f32[5]{0:T(128)} %thr_h.1, f32[5,32,16,128]{3,2,1,0:T(8,128)} %state_h.1, ...), custom_call_target="tpu_custom_call" | custom-call | tf_op jit(solution)/shard_map/pallas_call | solution.py:348
  20.3 1.5 %shard_map.105 = (f32[5,32,16,128]{3,2,1,0:T(8,128)}, f32[5,32,16,128]{3,2,1,0:T(8,128)}) custom-call(f32[5,32,16,128]{3,2,1,0:T(8,128)S(1)} %get-tuple-element.7.u0, f32[5,32,16,128]{3,2,1,0:T(8,128)S(1)} %get-tuple-element.8.rr, f32[5,32,16,128]{3,2,1,0:T(8,128)S(1)} %get-tuple-element.9.vv, f32[5,32,16,128]{3,2,1,0:T(8,128)S(1)} %get-tuple-element.10.fo, ...), custom_call_target="tpu_custom_call" | custom-call | tf_op jit(solution)/shard_map/pallas_call | solution.py:387

commit v3 on v2

--- a/solution.py
+++ b/solution.py
@@ -13,16 +13,27 @@
 US = 2
 UB = 2
 HALF = (slice(0, 8), slice(8, 16))
+NXC = NYC = 4
+SOLVERS = (
+    ((0, 1), (3, 1), (12, 1), (15, 1), (4, 1), (8, 1), (7, 1), (11, 1), (13, 1), (1, 1)),
+    ((5, 1), (6, 1), (9, 1), (10, 1), (2, 1), (14, 1), (4, 0), (8, 0), (7, 0), (1, 0)),
+)
+ORDER = (0, 1, 4, 3, 12, 2, 8, 5, 13, 7, 6, 9, 15, 14, 11, 10)
 
 
 def planes(begin, count, unroll, body, carry, down=False):
+    def one(z, carry):
+        return body(begin - z if down else begin + z, carry)
+
     def some(i, carry):
         for j in range(unroll):
-            z = i * unroll + j
-            carry = body(begin - z if down else begin + z, carry)
+            carry = one(i * unroll + j, carry)
         return carry
 
-    return lax.fori_loop(0, count // unroll, some, carry)
+    carry = lax.fori_loop(0, count // unroll, some, carry)
+    for z in range(count - count % unroll, count):
+        carry = one(z, carry)
+    return carry
 
 
 def tiles(fn):
@@ -33,16 +44,18 @@
     visc_h, coup_h, thr_h, state_h, forcing_h, mask_h, binv_h, lower_h, upper_h,
     u0, rr, vv, fo, ret,
     st, mk, bi, lo, up, gl, gu, qg, pp, sw,
-    visc, coup, thr, xs, xh, zh, acd_s, acd_r, be_s, be_r, ret_s, ret_r,
+    visc, coup, thr, xs, xh, zh, low, acd_s, acd_r, be_s, be_r, ret_s, ret_r,
     small_sem, load_sem, binv_sem, halo_ssem, halo_rsem,
-    acd_ssem, acd_rsem, be_ssem, be_rsem, ret_ssem, ret_rsem,
+    acd_ssem, acd_rsem, be_ssem, be_rsem, ret_ssem, ret_rsem, row_sem, pair_sem,
 ):
     n_line = lax.axis_size("line")
     n_blk = lax.axis_size("blk")
     me = lax.axis_index("line")
     mb = lax.axis_index("blk")
+    x, y, core = me // NYC, me % NYC, mb % 2
     depth = lo.shape[1]
     step = depth // CH
+    half = depth // 2
 
     copy = pltpu.make_async_copy
     ld_state = copy(state_h, st.at[:, pl.ds(1, depth)], load_sem.at[0])
@@ -67,21 +80,29 @@
     ld_lower.start()
     ld_upper.start()
 
-    def ahead(d):
-        j = me + d
-        return jnp.where(j >= n_line, j - n_line, j)
-
+    has_low, has_high = me > 0, me < n_line - 1
+    has_left, has_right = mb > 0, mb < n_blk - 1
+    turn_low = jnp.logical_and(has_low, y == 0)
+    turn_high = jnp.logical_and(has_high, y == NYC - 1)
     barrier = pltpu.get_barrier_semaphore()
-    for d in range(1, n_line):
-        pl.semaphore_signal(barrier, inc=1, device_id={"line": ahead(d)})
-
-    @pl.when(mb > 0)
-    def _():
-        pl.semaphore_signal(barrier, inc=1, device_id={"blk": mb - 1})
-
-    @pl.when(mb < n_blk - 1)
-    def _():
-        pl.semaphore_signal(barrier, inc=1, device_id={"blk": mb + 1})
+
+    def greet(**device):
+        pl.semaphore_signal(barrier, inc=1, device_id=device)
+
+    def wrap(v, n):
+        return jnp.where(v >= n, v - n, v)
+
+    def in_column(d):
+        return wrap(x + d, NXC) * NYC + y
+
+    pl.when(has_left)(lambda: greet(blk=mb - 1))
+    pl.when(has_right)(lambda: greet(blk=mb + 1))
+    pl.when(turn_low)(lambda: greet(line=me - 1))
+    pl.when(turn_high)(lambda: greet(line=me + 1))
+    for d in range(1, NYC):
+        greet(line=x * NYC + wrap(y + d, NYC))
+    for d in range(1, NXC):
+        greet(line=in_column(d))
 
     for k in range(CH):
         ld_binv(k).start()
@@ -92,14 +113,17 @@
         for sub in HALF:
             st[c, 0, sub, :] = zero_tile
             st[c, depth + 1, sub, :] = zero_tile
+            sw[c, 0, sub, :] = zero_tile
 
     ld_state.wait()
     for c in range(F):
         for side, row in ((0, 0), (1, 15)):
             xs[side, c] = st[c, 1 : depth + 1, row, :]
 
-    beside_blk = jnp.where(mb > 0, 1, 0) + jnp.where(mb < n_blk - 1, 1, 0)
-    pl.semaphore_wait(barrier, n_line - 1 + beside_blk)
+    greeted = NYC - 1 + NXC - 1
+    for cond in (has_left, has_right, turn_low, turn_high):
+        greeted = greeted + jnp.where(cond, 1, 0)
+    pl.semaphore_wait(barrier, greeted)
 
     def z_send(side):
         return pltpu.make_async_remote_copy(
@@ -108,23 +132,27 @@
             device_id={"line": me + 1 if side else me - 1},
         )
 
-    def x_send(side):
+    def x_send(side, part):
+        zs = pl.ds(part * half, half)
         return pltpu.make_async_remote_copy(
-            src_ref=xs.at[side], dst_ref=xh.at[1 - side],
-            send_sem=halo_ssem.at[2 + side], recv_sem=halo_rsem.at[2 + side],
+            src_ref=xs.at[side, :, zs], dst_ref=xh.at[1 - side, :, zs],
+            send_sem=halo_ssem.at[2 + 2 * part + side], recv_sem=halo_rsem.at[2 + 2 * part + side],
             device_id={"blk": mb + 1 if side else mb - 1},
         )
 
-    has_low, has_high = me > 0, me < n_line - 1
-    has_left, has_right = mb > 0, mb < n_blk - 1
-    halos = (
-        (has_left, x_send(0), x_send(1)),
-        (has_right, x_send(1), x_send(0)),
-        (has_low, z_send(0), z_send(1)),
-        (has_high, z_send(1), z_send(0)),
+    outgoing = (
+        (has_low, z_send(0)),
+        (has_high, z_send(1)),
+        (has_left, x_send(0, 0)),
+        (has_right, x_send(1, 0)),
+        (has_left, x_send(0, 1)),
+        (has_right, x_send(1, 1)),
     )
-    for cond, out, _ in halos:
+    for cond, out in outgoing:
         pl.when(cond)(out.start)
+
+    for d in range(1, NXC):
+        pl.semaphore_signal(row_sem, inc=1, device_id={"line": in_column(d)})
 
     ld_forcing.wait()
     ld_mask.wait()
@@ -165,6 +193,11 @@
 
     ld_lower.wait()
     ld_upper.wait()
+    for c in range(F):
+        for h, sub in enumerate(HALF):
+            low[c, h] = lo[c, 0, sub, :]
+            lo[c, 0, sub, :] = one_tile
+
 
     def decay_plane(z, carry):
         new = []
@@ -184,68 +217,107 @@
         return tuple(new)
 
     acd = planes(0, depth, UE, decay_plane, ((one_tile, one_tile, zero_tile),) * NV)
-    for v in range(NV):
-        for i in range(3):
-            acd_s[v, i] = acd[v][i]
-
-    def to_solvers(src, dst, ssem, rsem):
-        for d in range(1, n_line):
-            j = ahead(d)
-
-            @pl.when(j < NV)
-            def _():
-                pltpu.make_async_remote_copy(
-                    src_ref=src.at[j], dst_ref=dst.at[me], send_sem=ssem, recv_sem=rsem,
-                    device_id={"line": j},
-                ).start()
+    for c in range(F):
+        for h, sub in enumerate(HALF):
+            l2 = 1.0 - low[c, h] * low[c, h]
+            gl[c, 0, sub, :] = l2 * lax.rsqrt(l2)
+            p, q, r = acd[2 * c + h]
+            acd_s[2 * c + h, 0] = p * low[c, h]
+            acd_s[2 * c + h, 1] = q
+            acd_s[2 * c + h, 2] = r * low[c, h]
+
+    pl.semaphore_wait(row_sem, NXC - 1)
+
+    other = mb + 1 - 2 * core
+    pl.semaphore_signal(pair_sem, inc=1, device_id={"blk": other})
+    pl.semaphore_wait(pair_sem, 1)
 
     def drain(ref, sem):
         copy(ref, ref, sem).wait()
 
+    def to_solvers(src, dst, ssem, rsem):
+        for mine in range(2):
+
+            @pl.when(core == mine)
+            def _():
+                for v, (line, at) in enumerate(SOLVERS[mine]):
+                    out = pltpu.make_async_remote_copy(
+                        src_ref=src.at[v], dst_ref=dst.at[me], send_sem=ssem, recv_sem=rsem,
+                        device_id={"line": line, "blk": mb if at == mine else other},
+                    )
+                    if at == mine:
+                        pl.when(me != line)(out.start)
+                    else:
+                        out.start()
+
     to_solvers(acd_s, acd_r, acd_ssem, acd_rsem)
 
-    pl.when(has_left)(halos[0][2].wait_recv)
-    pl.when(has_right)(halos[1][2].wait_recv)
-    pl.when(has_low)(halos[2][2].wait_recv)
-    pl.when(has_high)(halos[3][2].wait_recv)
-
-    def add_x(side, row):
-        for c in range(F):
-            fo[c, :, row, :] = fo[c, :, row, :] + vis[c] * xh[side, c]
-
-    def add_z(side, z):
-        for c in range(F):
-            fo[c, z] = fo[c, z] + vis[c] * zh[side, c]
-
-    pl.when(has_left)(lambda: add_x(0, 0))
-    pl.when(has_right)(lambda: add_x(1, 15))
-    pl.when(has_low)(lambda: add_z(0, 0))
-    pl.when(has_high)(lambda: add_z(1, depth - 1))
+    def source(z, i):
+        c, sub = i // 2, HALF[i % 2]
+        src = bi[c, 0, z, sub, :] * fo[0, z, sub, :]
+        for d in range(1, F):
+            src = src + bi[c, d, z, sub, :] * fo[d, z, sub, :]
+        return gl[c, z, sub, :] * src
 
     def sweep_plane(z, carry):
         s, e = carry
         new_s, new_e = [], []
         for i in range(NV):
             c, sub = i // 2, HALF[i % 2]
-            src = bi[c, 0, z, sub, :] * fo[0, z, sub, :]
-            for d in range(1, F):
-                src = src + bi[c, d, z, sub, :] * fo[d, z, sub, :]
-            v = lo[c, z, sub, :] * s[i] + gl[c, z, sub, :] * src
+            v = lo[c, z, sub, :] * s[i] + source(z, i)
             sw[c, z, sub, :] = v
             new_s.append(v)
             new_e.append(e[i] + qg[c, z, sub, :] * v)
         return tuple(new_s), tuple(new_e)
 
+    def add_x(side, part, row):
+        zs = slice(part * half, part * half + half)
+        for c in range(F):
+            fo[c, zs, row, :] = fo[c, zs, row, :] + vis[c] * xh[side, c, zs]
+
+    def add_z(side, z):
+        for c in range(F):
+            fo[c, z] = fo[c, z] + vis[c] * zh[side, c]
+
+    def x_halo(part):
+        @pl.when(has_left)
+        def _():
+            x_send(1, part).wait_recv()
+            add_x(0, part, 0)
+
+        @pl.when(has_right)
+        def _():
+            x_send(0, part).wait_recv()
+            add_x(1, part, 15)
+
     carry = ((zero_tile,) * NV, (zero_tile,) * NV)
-
-    def sweep_chunk(k, carry):
+    for k in range(CH):
+        if k * step % half == 0:
+            x_halo(k * step // half)
         ld_binv(k).wait()
-        return planes(k * step, step, US, sweep_plane, carry)
-
-    b_all, e_all = lax.fori_loop(0, CH, sweep_chunk, carry)
-    for v in range(NV):
-        be_s[v, 0] = b_all[v]
-        be_s[v, 1] = e_all[v]
+        begin = max(k * step, 1)
+        end = min((k + 1) * step, depth - 1)
+        carry = planes(begin, end - begin, US, sweep_plane, carry)
+
+    @pl.when(has_high)
+    def _():
+        z_send(0).wait_recv()
+        add_z(1, depth - 1)
+
+    s_all, e_all = sweep_plane(depth - 1, carry)
+
+    @pl.when(has_low)
+    def _():
+        z_send(1).wait_recv()
+        add_z(0, 0)
+
+    for i in range(NV):
+        c, h = i // 2, i % 2
+        p, q, r = acd[i]
+        s0 = source(0, i)
+        be_s[i, 0] = s_all[i] + p * s0
+        be_s[i, 1] = e_all[i] + r * s0
+        ret[c, h, 0] = s0
     to_solvers(be_s, be_r, be_ssem, be_rsem)
 
     def down_plane(z, carry):
@@ -264,12 +336,23 @@
 
     planes(depth - 1, depth, UB, down_plane, ((zero_tile, zero_tile, one_tile),) * NV, down=True)
 
-    @pl.when(me < NV)
-    def _():
-        acd_r[me] = acd_s[me]
-        be_r[me] = be_s[me]
-        drain(acd_r.at[pl.ds(0, n_line - 1)], acd_rsem)
-        drain(be_r.at[pl.ds(0, n_line - 1)], be_rsem)
+    def role(cross):
+        found, tile = False, 0
+        for mine in range(2):
+            for v, (line, at) in enumerate(SOLVERS[mine]):
+                if (at != mine) == cross:
+                    here = jnp.logical_and(core == at, me == line)
+                    found = jnp.logical_or(found, here)
+                    tile = jnp.where(here, v, tile)
+        return found, tile
+
+    def solve(tile, cross):
+        count = n_line if cross else n_line - 1
+        if not cross:
+            acd_r[me] = acd_s[tile]
+            be_r[me] = be_s[tile]
+        drain(acd_r.at[pl.ds(0, count)], acd_rsem)
+        drain(be_r.at[pl.ds(0, count)], be_rsem)
         s = zero_tile
         t = []
         for k in range(n_line):
@@ -280,29 +363,46 @@
         for k in range(n_line - 1, -1, -1):
             ret_s[k, 1] = u
             u = acd_r[k, 1] * u + t[k]
-        for d in range(1, n_line):
-            k = ahead(d)
-            pltpu.make_async_remote_copy(
-                src_ref=ret_s.at[k], dst_ref=ret_r.at[me], send_sem=ret_ssem, recv_sem=ret_rsem,
-                device_id={"line": k},
-            ).start()
-        ret_r[me] = ret_s[me]
+        for k in ORDER:
+            out = pltpu.make_async_remote_copy(
+                src_ref=ret_s.at[k], dst_ref=ret_r.at[tile], send_sem=ret_ssem, recv_sem=ret_rsem,
+                device_id={"line": k, "blk": other if cross else mb},
+            )
+            if cross:
+                out.start()
+            else:
+                pl.when(me != k)(out.start)
+        if not cross:
+            ret_r[tile] = ret_s[me]
+
+    solves_other, other_tile = role(True)
+    solves_own, own_tile = role(False)
+
+    @pl.when(solves_other)
+    def _():
+        solve(other_tile, True)
+        drain(ret_s, ret_ssem)
+
+    @pl.when(solves_own)
+    def _():
+        solve(own_tile, False)
+        drain(ret_r.at[pl.ds(0, NV - 1)], ret_rsem)
+        drain(ret_s.at[pl.ds(0, n_line - 1)], ret_ssem)
         drain(acd_s.at[pl.ds(0, NV - 1)], acd_ssem)
         drain(be_s.at[pl.ds(0, NV - 1)], be_ssem)
-        drain(ret_s.at[pl.ds(0, n_line - 1)], ret_ssem)
-        drain(ret_r.at[pl.ds(0, NV - 1)], ret_rsem)
-
-    @pl.when(me >= NV)
+
+    @pl.when(jnp.logical_not(solves_own))
     def _():
+        drain(ret_r, ret_rsem)
         drain(acd_s, acd_ssem)
         drain(be_s, be_ssem)
-        drain(ret_r, ret_rsem)
-
-    for v in range(NV):
-        for i in range(2):
-            ret[v, i] = ret_r[v, i]
-
-    for cond, out, _ in halos:
+
+    for c in range(F):
+        for h in range(2):
+            ret[c, h, 0] = ret[c, h, 0] + low[c, h] * ret_r[2 * c + h, 0]
+            ret[c, h, 1] = ret_r[2 * c + h, 1]
+
+    for cond, out in outgoing:
         pl.when(cond)(out.wait_send)
 
 
@@ -316,8 +416,8 @@
         part = pl.ds(k * step, step)
         return pltpu.make_async_copy(out.at[:, part], update_h.at[:, part], out_sem.at[k])
 
-    s_in = tiles(lambda c, h: ret[2 * c + h, 0])
-    u_in = tiles(lambda c, h: ret[2 * c + h, 1])
+    s_in = tiles(lambda c, h: ret[c, h, 0])
+    u_in = tiles(lambda c, h: ret[c, h, 1])
 
     def plane(z, carry):
         for i in range(NV):
@@ -347,7 +447,7 @@
     args = (viscosity, coupling, thrust, state, forcing, disk_mask, block_inverse, lower_decay, upper_decay)
     parts = pl.pallas_call(
         segment_kernel,
-        out_shape=(V(full, f32),) * 4 + (V((NV, 2, 8, lanes), f32),),
+        out_shape=(V(full, f32),) * 4 + (V((fields, 2, 2, 8, lanes), f32),),
         in_specs=[hbm] * len(args),
         out_specs=(vmem,) * 5,
         scratch_shapes=[
@@ -367,6 +467,7 @@
             V((2, fields, depth, lanes), f32),
             V((2, fields, depth, lanes), f32),
             V((2, fields, width, lanes), f32),
+            V((fields, 2, 8, lanes), f32),
             V((NV, 3, 8, lanes), f32),
             V((n_line, 3, 8, lanes), f32),
             V((NV, 2, 8, lanes), f32),
@@ -376,9 +477,11 @@
             dma((3,)),
             dma((5,)),
             dma((CH,)),
-            dma((4,)),
-            dma((4,)),
+            dma((6,)),
+            dma((6,)),
             dma, dma, dma, dma, dma, dma,
+            pltpu.SemaphoreType.REGULAR,
+            pltpu.SemaphoreType.REGULAR,
         ],
         compiler_params=pltpu.CompilerParams(
             collective_id=0, has_side_effects=True, vmem_limit_bytes=40 * 1024 * 1024

time: 22.1 us -> 21.1 us (0.955)
  Pallas kernels: 21.2 us -> 20.4 us
    pallas_call x1, Pallas kernels: 19.7 us -> 18.8 us  [local(): pl.pallas_call(segment_kernel, out_shape=(V(full, f32),) * 4 + (V((fields...]
where the time goes in v3:
time: 21.1 us; the launch traced here: 21 us
  Pallas kernels  20.4 us (97%)
  between operations  0.64 us (3%)
    pallas_call x1, Pallas kernels, local(): pl.pallas_call(segment_kernel, out_shape=(V(full, f32),) * 4 + (V((fields...  18.8 us
    pallas_call x1, Pallas kernels, local(): pl.pallas_call(finish_kernel, out_shape=(pltpu.HBM(full, f32), pltpu.HBM(...  1.52 us

profile of v3, /device:TPU:1, one launch (start us, length us, event | category | flops | bytes accessed | tf_op | source)
XLA Modules:
  0.0 21.0 jit_solution(7045039224265081430)
XLA Ops:
  0.6 18.8 %shard_map.104 = (f32[5,32,16,128]{3,2,1,0:T(8,128)S(1)}, f32[5,32,16,128]{3,2,1,0:T(8,128)S(1)}, f32[5,32,16,128]{3,2,1,0:T(8,128)S(1)}, f32[5,32,16,128]{3,2,1,0:T(8,128)S(1)}, f32[5,2,2,8,128]{4,3,2,1,0:T(8,128)S(1)}) custom-call(f32[5]{0:T(128)} %visc_h.1, f32[5,5]{1,0:T(8,128)} %coup_h.1, f32[5]{0:T(128)} %thr_h.1, f32[5,32,16,128]{3,2,1,0:T(8,128)} %state_h.1, ...), custom_call_target="tpu_custom_call" | custom-call | tf_op jit(solution)/shard_map/pallas_call | solution.py:448
  19.5 1.5 %shard_map.105 = (f32[5,32,16,128]{3,2,1,0:T(8,128)}, f32[5,32,16,128]{3,2,1,0:T(8,128)}) custom-call(f32[5,32,16,128]{3,2,1,0:T(8,128)S(1)} %get-tuple-element.7.u0, f32[5,32,16,128]{3,2,1,0:T(8,128)S(1)} %get-tuple-element.8.rr, f32[5,32,16,128]{3,2,1,0:T(8,128)S(1)} %get-tuple-element.9.vv, f32[5,32,16,128]{3,2,1,0:T(8,128)S(1)} %get-tuple-element.10.fo, ...), custom_call_target="tpu_custom_call" | custom-call | tf_op jit(solution)/shard_map/pallas_call | solution.py:490

commit v4 on v3

--- a/solution.py
+++ b/solution.py
@@ -8,15 +8,18 @@
 F = 5
 NV = 2 * F
 CH = 4
-UE = 2
-UR = 2
-US = 2
-UB = 2
+XP = 1
+UE = 4
+UR = 8
+US = 4
+UB = 4
+UF = 2
+CF = 4
 HALF = (slice(0, 8), slice(8, 16))
 NXC = NYC = 4
 SOLVERS = (
-    ((0, 1), (3, 1), (12, 1), (15, 1), (4, 1), (8, 1), (7, 1), (11, 1), (13, 1), (1, 1)),
-    ((5, 1), (6, 1), (9, 1), (10, 1), (2, 1), (14, 1), (4, 0), (8, 0), (7, 0), (1, 0)),
+    ((0, 0), (3, 0), (4, 0), (12, 0), (9, 1), (5, 1), (13, 1), (6, 1), (10, 1), (14, 1)),
+    ((0, 1), (4, 1), (12, 1), (15, 1), (3, 1), (8, 1), (1, 1), (2, 1), (11, 1), (7, 1)),
 )
 ORDER = (0, 1, 4, 3, 12, 2, 8, 5, 13, 7, 6, 9, 15, 14, 11, 10)
 
@@ -55,7 +58,7 @@
     x, y, core = me // NYC, me % NYC, mb % 2
     depth = lo.shape[1]
     step = depth // CH
-    half = depth // 2
+    piece = depth // XP
 
     copy = pltpu.make_async_copy
     ld_state = copy(state_h, st.at[:, pl.ds(1, depth)], load_sem.at[0])
@@ -133,7 +136,7 @@
         )
 
     def x_send(side, part):
-        zs = pl.ds(part * half, half)
+        zs = pl.ds(part * piece, piece)
         return pltpu.make_async_remote_copy(
             src_ref=xs.at[side, :, zs], dst_ref=xh.at[1 - side, :, zs],
             send_sem=halo_ssem.at[2 + 2 * part + side], recv_sem=halo_rsem.at[2 + 2 * part + side],
@@ -143,10 +146,8 @@
     outgoing = (
         (has_low, z_send(0)),
         (has_high, z_send(1)),
-        (has_left, x_send(0, 0)),
-        (has_right, x_send(1, 0)),
-        (has_left, x_send(0, 1)),
-        (has_right, x_send(1, 1)),
+    ) + tuple(
+        (cond, x_send(side, part)) for part in range(XP) for side, cond in ((0, has_left), (1, has_right))
     )
     for cond, out in outgoing:
         pl.when(cond)(out.start)
@@ -271,7 +272,7 @@
         return tuple(new_s), tuple(new_e)
 
     def add_x(side, part, row):
-        zs = slice(part * half, part * half + half)
+        zs = slice(part * piece, part * piece + piece)
         for c in range(F):
             fo[c, zs, row, :] = fo[c, zs, row, :] + vis[c] * xh[side, c, zs]
 
@@ -292,8 +293,8 @@
 
     carry = ((zero_tile,) * NV, (zero_tile,) * NV)
     for k in range(CH):
-        if k * step % half == 0:
-            x_halo(k * step // half)
+        if k * step % piece == 0:
+            x_halo(k * step // piece)
         ld_binv(k).wait()
         begin = max(k * step, 1)
         end = min((k + 1) * step, depth - 1)
@@ -408,7 +409,7 @@
 
 def finish_kernel(u0, rr, vv, fo, ret, update_h, resid_h, out, res_sem, out_sem):
     depth = u0.shape[1]
-    step = depth // CH
+    step = depth // CF
     write_res = pltpu.make_async_copy(fo, resid_h, res_sem)
     write_res.start()
 
@@ -425,11 +426,11 @@
             out[c, z, sub, :] = u0[c, z, sub, :] + rr[c, z, sub, :] * s_in[i] + vv[c, z, sub, :] * u_in[i]
         return carry
 
-    for k in range(CH):
-        planes(k * step, step, 2, plane, 0)
+    for k in range(CF):
+        planes(k * step, step, UF, plane, 0)
         update_copy(k).start()
     write_res.wait()
-    for k in range(CH):
+    for k in range(CF):
         update_copy(k).wait()
 
 
@@ -476,9 +477,9 @@
             V((NV, 2, 8, lanes), f32),
             dma((3,)),
             dma((5,)),
-            dma((CH,)),
-            dma((6,)),
-            dma((6,)),
+            dma((CF,)),
+            dma((2 + 2 * XP,)),
+            dma((2 + 2 * XP,)),
             dma, dma, dma, dma, dma, dma,
             pltpu.SemaphoreType.REGULAR,
             pltpu.SemaphoreType.REGULAR,
@@ -492,7 +493,7 @@
         out_shape=(pltpu.HBM(full, f32), pltpu.HBM(full, f32)),
         in_specs=[vmem] * 5,
         out_specs=(hbm, hbm),
-        scratch_shapes=[V(full, f32), dma, dma((CH,))],
+        scratch_shapes=[V(full, f32), dma, dma((CF,))],
         compiler_params=pltpu.CompilerParams(vmem_limit_bytes=16 * 1024 * 1024),
     )(*(pltpu.with_memory_space_constraint(x, pltpu.VMEM) for x in parts))
 

time: 21.1 us -> 20.5 us (0.972)
  Pallas kernels: 20.4 us -> 19.7 us
    pallas_call x1, Pallas kernels: 18.8 us -> 18.2 us  [local(): pl.pallas_call(segment_kernel, out_shape=(V(full, f32),) * 4 + (V((fields...]
where the time goes in v4:
time: 20.5 us; the launch traced here: 20.3 us
  Pallas kernels  19.7 us (96%)
  between operations  0.64 us (3%)
    pallas_call x1, Pallas kernels, local(): pl.pallas_call(segment_kernel, out_shape=(V(full, f32),) * 4 + (V((fields...  18.2 us
    pallas_call x1, Pallas kernels, local(): pl.pallas_call(finish_kernel, out_shape=(pltpu.HBM(full, f32), pltpu.HBM(...  1.52 us

profile of v4, /device:TPU:1, one launch (start us, length us, event | category | flops | bytes accessed | tf_op | source)
XLA Modules:
  0.0 20.3 jit_solution(3035231038285154127)
XLA Ops:
  0.6 18.2 %shard_map.104 = (f32[5,32,16,128]{3,2,1,0:T(8,128)S(1)}, f32[5,32,16,128]{3,2,1,0:T(8,128)S(1)}, f32[5,32,16,128]{3,2,1,0:T(8,128)S(1)}, f32[5,32,16,128]{3,2,1,0:T(8,128)S(1)}, f32[5,2,2,8,128]{4,3,2,1,0:T(8,128)S(1)}) custom-call(f32[5]{0:T(128)} %visc_h.1, f32[5,5]{1,0:T(8,128)} %coup_h.1, f32[5]{0:T(128)} %thr_h.1, f32[5,32,16,128]{3,2,1,0:T(8,128)} %state_h.1, ...), custom_call_target="tpu_custom_call" | custom-call | tf_op jit(solution)/shard_map/pallas_call | solution.py:449
  18.8 1.5 %shard_map.105 = (f32[5,32,16,128]{3,2,1,0:T(8,128)}, f32[5,32,16,128]{3,2,1,0:T(8,128)}) custom-call(f32[5,32,16,128]{3,2,1,0:T(8,128)S(1)} %get-tuple-element.7.u0, f32[5,32,16,128]{3,2,1,0:T(8,128)S(1)} %get-tuple-element.8.rr, f32[5,32,16,128]{3,2,1,0:T(8,128)S(1)} %get-tuple-element.9.vv, f32[5,32,16,128]{3,2,1,0:T(8,128)S(1)} %get-tuple-element.10.fo, ...), custom_call_target="tpu_custom_call" | custom-call | tf_op jit(solution)/shard_map/pallas_call | solution.py:491

commit v5 on v4

--- a/solution.py
+++ b/solution.py
@@ -8,7 +8,6 @@
 F = 5
 NV = 2 * F
 CH = 4
-XP = 1
 UE = 4
 UR = 8
 US = 4
@@ -18,7 +17,7 @@
 HALF = (slice(0, 8), slice(8, 16))
 NXC = NYC = 4
 SOLVERS = (
-    ((0, 0), (3, 0), (4, 0), (12, 0), (9, 1), (5, 1), (13, 1), (6, 1), (10, 1), (14, 1)),
+    ((3, 1), (12, 1), (9, 1), (5, 1), (13, 1), (6, 1), (8, 0), (7, 0), (0, 0), (4, 0)),
     ((0, 1), (4, 1), (12, 1), (15, 1), (3, 1), (8, 1), (1, 1), (2, 1), (11, 1), (7, 1)),
 )
 ORDER = (0, 1, 4, 3, 12, 2, 8, 5, 13, 7, 6, 9, 15, 14, 11, 10)
@@ -58,7 +57,6 @@
     x, y, core = me // NYC, me % NYC, mb % 2
     depth = lo.shape[1]
     step = depth // CH
-    piece = depth // XP
 
     copy = pltpu.make_async_copy
     ld_state = copy(state_h, st.at[:, pl.ds(1, depth)], load_sem.at[0])
@@ -78,10 +76,10 @@
     ld_state.start()
     for cp in ld_small:
         cp.start()
+    ld_lower.start()
+    ld_upper.start()
     ld_forcing.start()
     ld_mask.start()
-    ld_lower.start()
-    ld_upper.start()
 
     has_low, has_high = me > 0, me < n_line - 1
     has_left, has_right = mb > 0, mb < n_blk - 1
@@ -135,25 +133,59 @@
             device_id={"line": me + 1 if side else me - 1},
         )
 
-    def x_send(side, part):
-        zs = pl.ds(part * piece, piece)
+    def x_send(side):
         return pltpu.make_async_remote_copy(
-            src_ref=xs.at[side, :, zs], dst_ref=xh.at[1 - side, :, zs],
-            send_sem=halo_ssem.at[2 + 2 * part + side], recv_sem=halo_rsem.at[2 + 2 * part + side],
+            src_ref=xs.at[side], dst_ref=xh.at[1 - side],
+            send_sem=halo_ssem.at[2 + side], recv_sem=halo_rsem.at[2 + side],
             device_id={"blk": mb + 1 if side else mb - 1},
         )
 
     outgoing = (
         (has_low, z_send(0)),
         (has_high, z_send(1)),
-    ) + tuple(
-        (cond, x_send(side, part)) for part in range(XP) for side, cond in ((0, has_left), (1, has_right))
+        (has_left, x_send(0)),
+        (has_right, x_send(1)),
     )
     for cond, out in outgoing:
         pl.when(cond)(out.start)
 
     for d in range(1, NXC):
         pl.semaphore_signal(row_sem, inc=1, device_id={"line": in_column(d)})
+
+    ld_lower.wait()
+    ld_upper.wait()
+    for c in range(F):
+        for h, sub in enumerate(HALF):
+            low[c, h] = lo[c, 0, sub, :]
+            lo[c, 0, sub, :] = one_tile
+
+
+    def decay_plane(z, carry):
+        new = []
+        for i, (p, q, r) in enumerate(carry):
+            c, sub = i // 2, HALF[i % 2]
+            l, u = lo[c, z, sub, :], up[c, z, sub, :]
+            l2 = 1.0 - l * l
+            u2 = 1.0 - u * u
+            g = u2 * lax.rsqrt(u2)
+            gl[c, z, sub, :] = l2 * lax.rsqrt(l2)
+            gu[c, z, sub, :] = g
+            p = p * l
+            w = q * g
+            pp[c, z, sub, :] = p
+            qg[c, z, sub, :] = w
+            new.append((p, q * u, r + w * p))
+        return tuple(new)
+
+    acd = planes(0, depth, UE, decay_plane, ((one_tile, one_tile, zero_tile),) * NV)
+    for c in range(F):
+        for h, sub in enumerate(HALF):
+            l2 = 1.0 - low[c, h] * low[c, h]
+            gl[c, 0, sub, :] = l2 * lax.rsqrt(l2)
+            p, q, r = acd[2 * c + h]
+            acd_s[2 * c + h, 0] = p * low[c, h]
+            acd_s[2 * c + h, 1] = q
+            acd_s[2 * c + h, 2] = r * low[c, h]
 
     ld_forcing.wait()
     ld_mask.wait()
@@ -190,42 +222,7 @@
                 fo[c, z, sub, :] = total
         return carry
 
-    planes(0, depth, UR, residual_plane, 0)
-
-    ld_lower.wait()
-    ld_upper.wait()
-    for c in range(F):
-        for h, sub in enumerate(HALF):
-            low[c, h] = lo[c, 0, sub, :]
-            lo[c, 0, sub, :] = one_tile
-
-
-    def decay_plane(z, carry):
-        new = []
-        for i, (p, q, r) in enumerate(carry):
-            c, sub = i // 2, HALF[i % 2]
-            l, u = lo[c, z, sub, :], up[c, z, sub, :]
-            l2 = 1.0 - l * l
-            u2 = 1.0 - u * u
-            g = u2 * lax.rsqrt(u2)
-            gl[c, z, sub, :] = l2 * lax.rsqrt(l2)
-            gu[c, z, sub, :] = g
-            p = p * l
-            w = q * g
-            pp[c, z, sub, :] = p
-            qg[c, z, sub, :] = w
-            new.append((p, q * u, r + w * p))
-        return tuple(new)
-
-    acd = planes(0, depth, UE, decay_plane, ((one_tile, one_tile, zero_tile),) * NV)
-    for c in range(F):
-        for h, sub in enumerate(HALF):
-            l2 = 1.0 - low[c, h] * low[c, h]
-            gl[c, 0, sub, :] = l2 * lax.rsqrt(l2)
-            p, q, r = acd[2 * c + h]
-            acd_s[2 * c + h, 0] = p * low[c, h]
-            acd_s[2 * c + h, 1] = q
-            acd_s[2 * c + h, 2] = r * low[c, h]
+    planes(0, depth // 2, UR, residual_plane, 0)
 
     pl.semaphore_wait(row_sem, NXC - 1)
 
@@ -243,7 +240,8 @@
             def _():
                 for v, (line, at) in enumerate(SOLVERS[mine]):
                     out = pltpu.make_async_remote_copy(
-                        src_ref=src.at[v], dst_ref=dst.at[me], send_sem=ssem, recv_sem=rsem,
+                        src_ref=src.at[v], dst_ref=dst.at[int(at == mine), me], send_sem=ssem,
+                        recv_sem=rsem.at[int(at == mine)],
                         device_id={"line": line, "blk": mb if at == mine else other},
                     )
                     if at == mine:
@@ -253,72 +251,76 @@
 
     to_solvers(acd_s, acd_r, acd_ssem, acd_rsem)
 
-    def source(z, i):
-        c, sub = i // 2, HALF[i % 2]
+    planes(depth // 2, depth // 2, UR, residual_plane, 0)
+
+    def source(z, c, sub):
         src = bi[c, 0, z, sub, :] * fo[0, z, sub, :]
         for d in range(1, F):
             src = src + bi[c, d, z, sub, :] * fo[d, z, sub, :]
         return gl[c, z, sub, :] * src
 
-    def sweep_plane(z, carry):
-        s, e = carry
-        new_s, new_e = [], []
-        for i in range(NV):
-            c, sub = i // 2, HALF[i % 2]
-            v = lo[c, z, sub, :] * s[i] + source(z, i)
+    def sweep_plane(z, carry, sub):
+        new = []
+        for c, (s, e) in enumerate(carry):
+            v = lo[c, z, sub, :] * s + source(z, c, sub)
             sw[c, z, sub, :] = v
-            new_s.append(v)
-            new_e.append(e[i] + qg[c, z, sub, :] * v)
-        return tuple(new_s), tuple(new_e)
-
-    def add_x(side, part, row):
-        zs = slice(part * piece, part * piece + piece)
+            new.append((v, e + qg[c, z, sub, :] * v))
+        return tuple(new)
+
+    def add_x(side, row):
         for c in range(F):
-            fo[c, zs, row, :] = fo[c, zs, row, :] + vis[c] * xh[side, c, zs]
+            fo[c, :, row, :] = fo[c, :, row, :] + vis[c] * xh[side, c]
 
     def add_z(side, z):
         for c in range(F):
             fo[c, z] = fo[c, z] + vis[c] * zh[side, c]
 
-    def x_halo(part):
-        @pl.when(has_left)
+    def sweep_half(turn, unused):
+        h = jnp.where(core == 1, turn, 1 - turn)
+        sub = pl.ds(pl.multiple_of(8 * h, 8), 8)
+
+        @pl.when(jnp.logical_and(h == 0, has_left))
         def _():
-            x_send(1, part).wait_recv()
-            add_x(0, part, 0)
-
-        @pl.when(has_right)
+            x_send(1).wait_recv()
+            add_x(0, 0)
+
+        @pl.when(jnp.logical_and(h == 1, has_right))
         def _():
-            x_send(0, part).wait_recv()
-            add_x(1, part, 15)
-
-    carry = ((zero_tile,) * NV, (zero_tile,) * NV)
-    for k in range(CH):
-        if k * step % piece == 0:
-            x_halo(k * step // piece)
-        ld_binv(k).wait()
-        begin = max(k * step, 1)
-        end = min((k + 1) * step, depth - 1)
-        carry = planes(begin, end - begin, US, sweep_plane, carry)
+            x_send(0).wait_recv()
+            add_x(1, 15)
+
+        carry = ((zero_tile, zero_tile),) * F
+        for k in range(CH):
+            pl.when(turn == 0)(ld_binv(k).wait)
+            begin = max(k * step, 1)
+            end = min((k + 1) * step, depth - 1)
+            carry = planes(begin, end - begin, US, lambda z, c: sweep_plane(z, c, sub), carry)
+        for c in range(F):
+            be_s[2 * c + h, 0] = carry[c][0]
+            be_s[2 * c + h, 1] = carry[c][1]
+        return unused
+
+    lax.fori_loop(0, 2, sweep_half, 0)
 
     @pl.when(has_high)
     def _():
         z_send(0).wait_recv()
         add_z(1, depth - 1)
 
-    s_all, e_all = sweep_plane(depth - 1, carry)
-
     @pl.when(has_low)
     def _():
         z_send(1).wait_recv()
         add_z(0, 0)
 
-    for i in range(NV):
-        c, h = i // 2, i % 2
-        p, q, r = acd[i]
-        s0 = source(0, i)
-        be_s[i, 0] = s_all[i] + p * s0
-        be_s[i, 1] = e_all[i] + r * s0
-        ret[c, h, 0] = s0
+    for h, sub in enumerate(HALF):
+        carry = tuple((be_s[2 * c + h, 0], be_s[2 * c + h, 1]) for c in range(F))
+        carry = sweep_plane(depth - 1, carry, sub)
+        for c in range(F):
+            p, q, r = acd[2 * c + h]
+            s0 = source(0, c, sub)
+            be_s[2 * c + h, 0] = carry[c][0] + p * s0
+            be_s[2 * c + h, 1] = carry[c][1] + r * s0
+            ret[c, h, 0] = s0
     to_solvers(be_s, be_r, be_ssem, be_rsem)
 
     def down_plane(z, carry):
@@ -348,25 +350,26 @@
         return found, tile
 
     def solve(tile, cross):
+        i = 0 if cross else 1
         count = n_line if cross else n_line - 1
         if not cross:
-            acd_r[me] = acd_s[tile]
-            be_r[me] = be_s[tile]
-        drain(acd_r.at[pl.ds(0, count)], acd_rsem)
-        drain(be_r.at[pl.ds(0, count)], be_rsem)
+            acd_r[i, me] = acd_s[tile]
+            be_r[i, me] = be_s[tile]
+        drain(acd_r.at[i, pl.ds(0, count)], acd_rsem.at[i])
+        drain(be_r.at[i, pl.ds(0, count)], be_rsem.at[i])
         s = zero_tile
         t = []
         for k in range(n_line):
-            ret_s[k, 0] = s
-            t.append(acd_r[k, 2] * s + be_r[k, 1])
-            s = acd_r[k, 0] * s + be_r[k, 0]
+            ret_s[i, k, 0] = s
+            t.append(acd_r[i, k, 2] * s + be_r[i, k, 1])
+            s = acd_r[i, k, 0] * s + be_r[i, k, 0]
         u = zero_tile
         for k in range(n_line - 1, -1, -1):
-            ret_s[k, 1] = u
-            u = acd_r[k, 1] * u + t[k]
+            ret_s[i, k, 1] = u
+            u = acd_r[i, k, 1] * u + t[k]
         for k in ORDER:
             out = pltpu.make_async_remote_copy(
-                src_ref=ret_s.at[k], dst_ref=ret_r.at[tile], send_sem=ret_ssem, recv_sem=ret_rsem,
+                src_ref=ret_s.at[i, k], dst_ref=ret_r.at[tile], send_sem=ret_ssem.at[i], recv_sem=ret_rsem,
                 device_id={"line": k, "blk": other if cross else mb},
             )
             if cross:
@@ -374,21 +377,22 @@
             else:
                 pl.when(me != k)(out.start)
         if not cross:
-            ret_r[tile] = ret_s[me]
+            ret_r[tile] = ret_s[i, me]
 
     solves_other, other_tile = role(True)
     solves_own, own_tile = role(False)
+
+    @pl.when(solves_own)
+    def _():
+        solve(own_tile, False)
 
     @pl.when(solves_other)
     def _():
         solve(other_tile, True)
-        drain(ret_s, ret_ssem)
 
     @pl.when(solves_own)
     def _():
-        solve(own_tile, False)
         drain(ret_r.at[pl.ds(0, NV - 1)], ret_rsem)
-        drain(ret_s.at[pl.ds(0, n_line - 1)], ret_ssem)
         drain(acd_s.at[pl.ds(0, NV - 1)], acd_ssem)
         drain(be_s.at[pl.ds(0, NV - 1)], be_ssem)
 
@@ -405,6 +409,8 @@
 
     for cond, out in outgoing:
         pl.when(cond)(out.wait_send)
+    pl.when(solves_other)(lambda: drain(ret_s.at[0], ret_ssem.at[0]))
+    pl.when(solves_own)(lambda: drain(ret_s.at[1, pl.ds(0, n_line - 1)], ret_ssem.at[1]))
 
 
 def finish_kernel(u0, rr, vv, fo, ret, update_h, resid_h, out, res_sem, out_sem):
@@ -470,17 +476,17 @@
             V((2, fields, width, lanes), f32),
             V((fields, 2, 8, lanes), f32),
             V((NV, 3, 8, lanes), f32),
-            V((n_line, 3, 8, lanes), f32),
+            V((2, n_line, 3, 8, lanes), f32),
             V((NV, 2, 8, lanes), f32),
-            V((n_line, 2, 8, lanes), f32),
-            V((n_line, 2, 8, lanes), f32),
+            V((2, n_line, 2, 8, lanes), f32),
+            V((2, n_line, 2, 8, lanes), f32),
             V((NV, 2, 8, lanes), f32),
             dma((3,)),
             dma((5,)),
             dma((CF,)),
-            dma((2 + 2 * XP,)),
-            dma((2 + 2 * XP,)),
-            dma, dma, dma, dma, dma, dma,
+            dma((4,)),
+            dma((4,)),
+            dma, dma((2,)), dma, dma((2,)), dma((2,)), dma,
             pltpu.SemaphoreType.REGULAR,
             pltpu.SemaphoreType.REGULAR,
         ],

time: 20.5 us -> 20.3 us (level)
  no operation moved by 1% of the time
where the time goes in v5:
time: 20.3 us; the launch traced here: 20.2 us
  Pallas kernels  19.6 us (97%)
  between operations  0.64 us (3%)
    pallas_call x1, Pallas kernels, local(): pl.pallas_call(segment_kernel, out_shape=(V(full, f32),) * 4 + (V((fields...  18 us
    pallas_call x1, Pallas kernels, local(): pl.pallas_call(finish_kernel, out_shape=(pltpu.HBM(full, f32), pltpu.HBM(...  1.52 us

profile of v5, /device:TPU:1, one launch (start us, length us, event | category | flops | bytes accessed | tf_op | source)
XLA Modules:
  0.0 20.2 jit_solution(14147668712184341805)
XLA Ops:
  0.6 18.0 %shard_map.104 = (f32[5,32,16,128]{3,2,1,0:T(8,128)S(1)}, f32[5,32,16,128]{3,2,1,0:T(8,128)S(1)}, f32[5,32,16,128]{3,2,1,0:T(8,128)S(1)}, f32[5,32,16,128]{3,2,1,0:T(8,128)S(1)}, f32[5,2,2,8,128]{4,3,2,1,0:T(8,128)S(1)}) custom-call(f32[5]{0:T(128)} %visc_h.1, f32[5,5]{1,0:T(8,128)} %coup_h.1, f32[5]{0:T(128)} %thr_h.1, f32[5,32,16,128]{3,2,1,0:T(8,128)} %state_h.1, ...), custom_call_target="tpu_custom_call" | custom-call | tf_op jit(solution)/shard_map/pallas_call | solution.py:455
  18.7 1.5 %shard_map.105 = (f32[5,32,16,128]{3,2,1,0:T(8,128)}, f32[5,32,16,128]{3,2,1,0:T(8,128)}) custom-call(f32[5,32,16,128]{3,2,1,0:T(8,128)S(1)} %get-tuple-element.7.u0, f32[5,32,16,128]{3,2,1,0:T(8,128)S(1)} %get-tuple-element.8.rr, f32[5,32,16,128]{3,2,1,0:T(8,128)S(1)} %get-tuple-element.9.vv, f32[5,32,16,128]{3,2,1,0:T(8,128)S(1)} %get-tuple-element.10.fo, ...), custom_call_target="tpu_custom_call" | custom-call | tf_op jit(solution)/shard_map/pallas_call | solution.py:497

commit v6 on v5

--- a/solution.py
+++ b/solution.py
@@ -83,8 +83,6 @@
 
     has_low, has_high = me > 0, me < n_line - 1
     has_left, has_right = mb > 0, mb < n_blk - 1
-    turn_low = jnp.logical_and(has_low, y == 0)
-    turn_high = jnp.logical_and(has_high, y == NYC - 1)
     barrier = pltpu.get_barrier_semaphore()
 
     def greet(**device):
@@ -98,12 +96,16 @@
 
     pl.when(has_left)(lambda: greet(blk=mb - 1))
     pl.when(has_right)(lambda: greet(blk=mb + 1))
-    pl.when(turn_low)(lambda: greet(line=me - 1))
-    pl.when(turn_high)(lambda: greet(line=me + 1))
+    pl.when(has_low)(lambda: greet(line=me - 1))
+    pl.when(has_high)(lambda: greet(line=me + 1))
+    second = mb + 1 - core
     for d in range(1, NYC):
-        greet(line=x * NYC + wrap(y + d, NYC))
-    for d in range(1, NXC):
-        greet(line=in_column(d))
+        greet(line=x * NYC + wrap(y + d, NYC), blk=second)
+
+    @pl.when(core == 1)
+    def _():
+        for d in range(1, NXC):
+            greet(line=in_column(d))
 
     for k in range(CH):
         ld_binv(k).start()
@@ -121,8 +123,8 @@
         for side, row in ((0, 0), (1, 15)):
             xs[side, c] = st[c, 1 : depth + 1, row, :]
 
-    greeted = NYC - 1 + NXC - 1
-    for cond in (has_left, has_right, turn_low, turn_high):
+    greeted = core * (2 * (NYC - 1) + NXC - 1)
+    for cond in (has_left, has_right, has_low, has_high):
         greeted = greeted + jnp.where(cond, 1, 0)
     pl.semaphore_wait(barrier, greeted)
 
@@ -149,8 +151,10 @@
     for cond, out in outgoing:
         pl.when(cond)(out.start)
 
-    for d in range(1, NXC):
-        pl.semaphore_signal(row_sem, inc=1, device_id={"line": in_column(d)})
+    @pl.when(core == 1)
+    def _():
+        for d in range(1, NXC):
+            pl.semaphore_signal(row_sem, inc=1, device_id={"line": in_column(d)})
 
     ld_lower.wait()
     ld_upper.wait()
@@ -224,11 +228,19 @@
 
     planes(0, depth // 2, UR, residual_plane, 0)
 
-    pl.semaphore_wait(row_sem, NXC - 1)
-
     other = mb + 1 - 2 * core
-    pl.semaphore_signal(pair_sem, inc=1, device_id={"blk": other})
-    pl.semaphore_wait(pair_sem, 1)
+
+    @pl.when(core == 1)
+    def _():
+        pl.semaphore_wait(row_sem, NXC - 1)
+        pl.semaphore_signal(pair_sem, inc=1, device_id={"blk": other})
+
+    planes(depth // 2, depth // 2, UR, residual_plane, 0)
+
+    @pl.when(core == 0)
+    def _():
+        pl.semaphore_wait(pair_sem, 1)
+
 
     def drain(ref, sem):
         copy(ref, ref, sem).wait()
@@ -250,8 +262,6 @@
                         out.start()
 
     to_solvers(acd_s, acd_r, acd_ssem, acd_rsem)
-
-    planes(depth // 2, depth // 2, UR, residual_plane, 0)
 
     def source(z, c, sub):
         src = bi[c, 0, z, sub, :] * fo[0, z, sub, :]

time: 20.3 us -> 20.1 us (level)
    pallas_call x1, Pallas kernels: 18 us -> 17.8 us  [local(): pl.pallas_call(segment_kernel, out_shape=(V(full, f32),) * 4 + (V((fields...]
where the time goes in v6:
time: 20.1 us; the launch traced here: 20 us
  Pallas kernels  19.4 us (97%)
  between operations  0.64 us (3%)
    pallas_call x1, Pallas kernels, local(): pl.pallas_call(segment_kernel, out_shape=(V(full, f32),) * 4 + (V((fields...  17.8 us
    pallas_call x1, Pallas kernels, local(): pl.pallas_call(finish_kernel, out_shape=(pltpu.HBM(full, f32), pltpu.HBM(...  1.52 us

profile of v6, /device:TPU:1, one launch (start us, length us, event | category | flops | bytes accessed | tf_op | source)
XLA Modules:
  0.0 20.0 jit_solution(14342853390904501548)
XLA Ops:
  0.6 17.8 %shard_map.104 = (f32[5,32,16,128]{3,2,1,0:T(8,128)S(1)}, f32[5,32,16,128]{3,2,1,0:T(8,128)S(1)}, f32[5,32,16,128]{3,2,1,0:T(8,128)S(1)}, f32[5,32,16,128]{3,2,1,0:T(8,128)S(1)}, f32[5,2,2,8,128]{4,3,2,1,0:T(8,128)S(1)}) custom-call(f32[5]{0:T(128)} %visc_h.1, f32[5,5]{1,0:T(8,128)} %coup_h.1, f32[5]{0:T(128)} %thr_h.1, f32[5,32,16,128]{3,2,1,0:T(8,128)} %state_h.1, ...), custom_call_target="tpu_custom_call" | custom-call | tf_op jit(solution)/shard_map/pallas_call | solution.py:465
  18.5 1.5 %shard_map.105 = (f32[5,32,16,128]{3,2,1,0:T(8,128)}, f32[5,32,16,128]{3,2,1,0:T(8,128)}) custom-call(f32[5,32,16,128]{3,2,1,0:T(8,128)S(1)} %get-tuple-element.7.u0, f32[5,32,16,128]{3,2,1,0:T(8,128)S(1)} %get-tuple-element.8.rr, f32[5,32,16,128]{3,2,1,0:T(8,128)S(1)} %get-tuple-element.9.vv, f32[5,32,16,128]{3,2,1,0:T(8,128)S(1)} %get-tuple-element.10.fo, ...), custom_call_target="tpu_custom_call" | custom-call | tf_op jit(solution)/shard_map/pallas_call | solution.py:507

commit v7 on v6

--- a/solution.py
+++ b/solution.py
@@ -7,10 +7,10 @@
 
 F = 5
 NV = 2 * F
-CH = 4
+CH = 2
 UE = 4
 UR = 8
-US = 4
+US = 5
 UB = 4
 UF = 2
 CF = 4
@@ -57,6 +57,7 @@
     x, y, core = me // NYC, me % NYC, mb % 2
     depth = lo.shape[1]
     step = depth // CH
+    half = depth // 2
 
     copy = pltpu.make_async_copy
     ld_state = copy(state_h, st.at[:, pl.ds(1, depth)], load_sem.at[0])
@@ -135,18 +136,21 @@
             device_id={"line": me + 1 if side else me - 1},
         )
 
-    def x_send(side):
+    def x_send(side, part):
+        zs = pl.ds(part * half, half)
         return pltpu.make_async_remote_copy(
-            src_ref=xs.at[side], dst_ref=xh.at[1 - side],
-            send_sem=halo_ssem.at[2 + side], recv_sem=halo_rsem.at[2 + side],
+            src_ref=xs.at[side, :, zs], dst_ref=xh.at[1 - side, :, zs],
+            send_sem=halo_ssem.at[2 + 2 * part + side], recv_sem=halo_rsem.at[2 + 2 * part + side],
             device_id={"blk": mb + 1 if side else mb - 1},
         )
 
     outgoing = (
         (has_low, z_send(0)),
         (has_high, z_send(1)),
-        (has_left, x_send(0)),
-        (has_right, x_send(1)),
+        (has_left, x_send(0, 0)),
+        (has_right, x_send(1, 0)),
+        (has_left, x_send(0, 1)),
+        (has_right, x_send(1, 1)),
     )
     for cond, out in outgoing:
         pl.when(cond)(out.start)
@@ -277,9 +281,10 @@
             new.append((v, e + qg[c, z, sub, :] * v))
         return tuple(new)
 
-    def add_x(side, row):
+    def add_x(side, part, row):
+        zs = slice(part * half, part * half + half)
         for c in range(F):
-            fo[c, :, row, :] = fo[c, :, row, :] + vis[c] * xh[side, c]
+            fo[c, zs, row, :] = fo[c, zs, row, :] + vis[c] * xh[side, c, zs]
 
     def add_z(side, z):
         for c in range(F):
@@ -289,18 +294,21 @@
         h = jnp.where(core == 1, turn, 1 - turn)
         sub = pl.ds(pl.multiple_of(8 * h, 8), 8)
 
-        @pl.when(jnp.logical_and(h == 0, has_left))
-        def _():
-            x_send(1).wait_recv()
-            add_x(0, 0)
-
-        @pl.when(jnp.logical_and(h == 1, has_right))
-        def _():
-            x_send(0).wait_recv()
-            add_x(1, 15)
+        def x_halo(part):
+            @pl.when(jnp.logical_and(h == 0, has_left))
+            def _():
+                x_send(1, part).wait_recv()
+                add_x(0, part, 0)
+
+            @pl.when(jnp.logical_and(h == 1, has_right))
+            def _():
+                x_send(0, part).wait_recv()
+                add_x(1, part, 15)
 
         carry = ((zero_tile, zero_tile),) * F
         for k in range(CH):
+            if k * step % half == 0:
+                x_halo(k * step // half)
             pl.when(turn == 0)(ld_binv(k).wait)
             begin = max(k * step, 1)
             end = min((k + 1) * step, depth - 1)
@@ -494,8 +502,8 @@
             dma((3,)),
             dma((5,)),
             dma((CF,)),
-            dma((4,)),
-            dma((4,)),
+            dma((6,)),
+            dma((6,)),
             dma, dma((2,)), dma, dma((2,)), dma((2,)), dma,
             pltpu.SemaphoreType.REGULAR,
             pltpu.SemaphoreType.REGULAR,

time: 20.1 us -> 19.9 us (0.990)
  no operation moved by 1% of the time
where the time goes in v7:
time: 19.9 us; the launch traced here: 19.8 us
  Pallas kernels  19.2 us (96%)
  between operations  0.64 us (3%)
    pallas_call x1, Pallas kernels, local(): pl.pallas_call(segment_kernel, out_shape=(V(full, f32),) * 4 + (V((fields...  17.7 us
    pallas_call x1, Pallas kernels, local(): pl.pallas_call(finish_kernel, out_shape=(pltpu.HBM(full, f32), pltpu.HBM(...  1.52 us

profile of v7, /device:TPU:1, one launch (start us, length us, event | category | flops | bytes accessed | tf_op | source)
XLA Modules:
  0.0 19.8 jit_solution(10503853148318245211)
XLA Ops:
  0.6 17.7 %shard_map.104 = (f32[5,32,16,128]{3,2,1,0:T(8,128)S(1)}, f32[5,32,16,128]{3,2,1,0:T(8,128)S(1)}, f32[5,32,16,128]{3,2,1,0:T(8,128)S(1)}, f32[5,32,16,128]{3,2,1,0:T(8,128)S(1)}, f32[5,2,2,8,128]{4,3,2,1,0:T(8,128)S(1)}) custom-call(f32[5]{0:T(128)} %visc_h.1, f32[5,5]{1,0:T(8,128)} %coup_h.1, f32[5]{0:T(128)} %thr_h.1, f32[5,32,16,128]{3,2,1,0:T(8,128)} %state_h.1, ...), custom_call_target="tpu_custom_call" | custom-call | tf_op jit(solution)/shard_map/pallas_call | solution.py:473
  18.3 1.5 %shard_map.105 = (f32[5,32,16,128]{3,2,1,0:T(8,128)}, f32[5,32,16,128]{3,2,1,0:T(8,128)}) custom-call(f32[5,32,16,128]{3,2,1,0:T(8,128)S(1)} %get-tuple-element.7.u0, f32[5,32,16,128]{3,2,1,0:T(8,128)S(1)} %get-tuple-element.8.rr, f32[5,32,16,128]{3,2,1,0:T(8,128)S(1)} %get-tuple-element.9.vv, f32[5,32,16,128]{3,2,1,0:T(8,128)S(1)} %get-tuple-element.10.fo, ...), custom_call_target="tpu_custom_call" | custom-call | tf_op jit(solution)/shard_map/pallas_call | solution.py:515

commit v8 on v7

--- a/solution.py
+++ b/solution.py
@@ -145,12 +145,12 @@
         )
 
     outgoing = (
-        (has_low, z_send(0)),
-        (has_high, z_send(1)),
         (has_left, x_send(0, 0)),
         (has_right, x_send(1, 0)),
         (has_left, x_send(0, 1)),
         (has_right, x_send(1, 1)),
+        (has_low, z_send(0)),
+        (has_high, z_send(1)),
     )
     for cond, out in outgoing:
         pl.when(cond)(out.start)

time: 19.9 us -> 19.9 us (level)
  no operation moved by 1% of the time
where the time goes in v8:
time: 19.9 us; the launch traced here: 19.8 us
  Pallas kernels  19.2 us (96%)
  between operations  0.64 us (3%)
    pallas_call x1, Pallas kernels, local(): pl.pallas_call(segment_kernel, out_shape=(V(full, f32),) * 4 + (V((fields...  17.7 us
    pallas_call x1, Pallas kernels, local(): pl.pallas_call(finish_kernel, out_shape=(pltpu.HBM(full, f32), pltpu.HBM(...  1.52 us

profile of v8, /device:TPU:1, one launch (start us, length us, event | category | flops | bytes accessed | tf_op | source)
XLA Modules:
  0.0 19.8 jit_solution(7004320041317025644)
XLA Ops:
  0.6 17.7 %shard_map.104 = (f32[5,32,16,128]{3,2,1,0:T(8,128)S(1)}, f32[5,32,16,128]{3,2,1,0:T(8,128)S(1)}, f32[5,32,16,128]{3,2,1,0:T(8,128)S(1)}, f32[5,32,16,128]{3,2,1,0:T(8,128)S(1)}, f32[5,2,2,8,128]{4,3,2,1,0:T(8,128)S(1)}) custom-call(f32[5]{0:T(128)} %visc_h.1, f32[5,5]{1,0:T(8,128)} %coup_h.1, f32[5]{0:T(128)} %thr_h.1, f32[5,32,16,128]{3,2,1,0:T(8,128)} %state_h.1, ...), custom_call_target="tpu_custom_call" | custom-call | tf_op jit(solution)/shard_map/pallas_call | solution.py:473
  18.3 1.5 %shard_map.105 = (f32[5,32,16,128]{3,2,1,0:T(8,128)}, f32[5,32,16,128]{3,2,1,0:T(8,128)}) custom-call(f32[5,32,16,128]{3,2,1,0:T(8,128)S(1)} %get-tuple-element.7.u0, f32[5,32,16,128]{3,2,1,0:T(8,128)S(1)} %get-tuple-element.8.rr, f32[5,32,16,128]{3,2,1,0:T(8,128)S(1)} %get-tuple-element.9.vv, f32[5,32,16,128]{3,2,1,0:T(8,128)S(1)} %get-tuple-element.10.fo, ...), custom_call_target="tpu_custom_call" | custom-call | tf_op jit(solution)/shard_map/pallas_call | solution.py:515
